TPU v7x, 32 devices: a whole 2x2x4 slice. The times are simulated.
32 devices in a mesh: dp: 8 (over z, x), mp: 4 (over y, core).
Axes of the slice: x: 2, y: 2, z: 4, core: 2. Of those that a mesh axis runs over, the one named last changes fastest.
Arguments:
- block_input: bfloat16 [24576, 1024], P(('dp', 'mp')), may hold values from -6 to 6
- sequence_lengths: int32 [8, 6], P('dp'), may hold values from 0 to 1024, as said below
- first_gain: float32 [1024], replicated, may hold values from 0.5 to 1.5
- first_shift: float32 [1024], replicated, may hold values from -3 to 3
- second_gain: float32 [1024], replicated, may hold values from 0.5 to 1.5
- second_shift: float32 [1024], replicated, may hold values from -3 to 3
- triple_weight: bfloat16 [1024, 3072], P(None, 'mp'), may hold values from -0.1875 to 0.1875
- triple_left: bfloat16 [1024, 128], replicated, may hold values from -0.1875 to 0.1875
- triple_right: bfloat16 [128, 3072], replicated, may hold values from -0.25 to 0.25
- output_weight: bfloat16 [1024, 1024], P('mp'), may hold values from -0.5 to 0.5
- output_left: bfloat16 [1024, 128], replicated, may hold values from -0.5 to 0.5
- output_right: bfloat16 [128, 1024], replicated, may hold values from -0.25 to 0.25
- expand_weight: bfloat16 [1024, 4096], P(None, 'mp'), may hold values from -0.1875 to 0.1875
- expand_left: bfloat16 [1024, 128], replicated, may hold values from -0.1875 to 0.1875
- expand_right: bfloat16 [128, 4096], replicated, may hold values from -0.25 to 0.25
- shrink_weight: bfloat16 [4096, 1024], P('mp'), may hold values from -0.09375 to 0.09375
- shrink_left: bfloat16 [4096, 128], replicated, may hold values from -0.09375 to 0.09375
- shrink_right: bfloat16 [128, 1024], replicated, may hold values from -0.25 to 0.25
- cotangent: bfloat16 [24576, 1024], P(('dp', 'mp')), may hold values from -6 to 6
Outputs:
- block_output: bfloat16 [24576, 1024], P(('dp', 'mp'))
- input_gradient: float32 [24576, 1024], P(('dp', 'mp'))
- first_gain_gradient: float32 [1024], replicated
- first_shift_gradient: float32 [1024], replicated
- second_gain_gradient: float32 [1024], replicated
- second_shift_gradient: float32 [1024], replicated
- triple_left_gradient: float32 [1024, 128], replicated
- triple_right_gradient: float32 [128, 3072], replicated
- output_left_gradient: float32 [1024, 128], replicated
- output_right_gradient: float32 [128, 1024], replicated
- expand_left_gradient: float32 [1024, 128], replicated
- expand_right_gradient: float32 [128, 4096], replicated
- shrink_left_gradient: float32 [4096, 128], replicated
- shrink_right_gradient: float32 [128, 1024], replicated
Inputs may be any that keep to these rules, and one draw needn't show every extreme that they name: `sequence_lengths`: row g lists the lengths of the sequences of group g in order, each 512 or 1024, then zeros; every row sums to 3072 and holds at least one sequence of 1024.
All inputs are finite; a program needn't handle non-finite values.
Results may differ from a plain program's by a relative error of at most 0.012.
The roundings to bfloat16 on the way count: a program that leaves them out, or rounds other values in their place, can miss the bound.
Values may be sent and summed in bfloat16 or wider, within the bound.
A program may use at most 256 MiB of HBM per device.

v0:
```python
import functools
import math

import jax
import jax.numpy as jnp
import numpy as np
from jax import lax
from jax.experimental import pallas as pl
from jax.experimental.pallas import tpu as pltpu
from jax.sharding import PartitionSpec as P

HEAD_DIM = 64
ROT = 16
SHORT = 512
TOK_GRP = 3072
SLOTS = 6
EPS = 1e-05
LANES = 128
MESH = pl.DeviceIdType.MESH
BF16 = jnp.bfloat16
F32 = jnp.float32
VMEM_LIMIT = 56 * 1024 * 1024
BRIEF = pl.CostEstimate(flops=1, bytes_accessed=1, transcendentals=0)


def dot_nn(former, latter):
    return lax.dot_general(
        former, latter, (((1,), (0,)), ((), ())), preferred_element_type=F32
    )


def dot_nt(former, latter):
    return lax.dot_general(
        former, latter, (((1,), (1,)), ((), ())), preferred_element_type=F32
    )


def dot_tn(former, latter):
    return lax.dot_general(
        former, latter, (((0,), (0,)), ((), ())), preferred_element_type=F32
    )


def find_flags(group_lengths):
    seq_ends = jnp.cumsum(group_lengths, dtype=jnp.int32)
    starts = seq_ends - group_lengths
    block_starts = jnp.arange(SLOTS, dtype=jnp.int32) * SHORT
    begins = jnp.any(
        (starts[None, :] == block_starts[:, None]) & (group_lengths[None, :] > 0), axis=1
    )
    return jnp.where(begins, 0, 1).astype(jnp.int32)


def rotary_tables():
    half = ROT // 2
    frequency = np.exp(
        np.arange(half, dtype=np.float32) * np.float32(-2.0 * math.log(10000.0) / ROT)
    ).astype(np.float32)
    angles = np.arange(2 * SHORT, dtype=np.float32)[:, None] * frequency[None, :]
    cosine = np.ones((2 * SHORT, LANES), np.float32)
    minus = np.zeros((2 * SHORT, LANES), np.float32)
    plus = np.zeros((2 * SHORT, LANES), np.float32)
    for base in range(0, LANES, HEAD_DIM):
        cosine[:, base : base + half] = np.cos(angles)
        cosine[:, base + half : base + ROT] = np.cos(angles)
        minus[:, base : base + half] = -np.sin(angles)
        plus[:, base + half : base + ROT] = np.sin(angles)
    return jnp.asarray(cosine), jnp.asarray(minus), jnp.asarray(plus)


def tall_tables():
    half = ROT // 2
    frequency = np.exp(
        np.arange(half, dtype=np.float32) * np.float32(-2.0 * math.log(10000.0) / ROT)
    ).astype(np.float32)
    angles = frequency[:, None] * np.arange(2 * SHORT, dtype=np.float32)[None, :]
    return jnp.asarray(np.cos(angles)), jnp.asarray(np.sin(angles))


def low_lanes():
    return lax.broadcasted_iota(jnp.int32, (1, LANES), 1) < HEAD_DIM


def rotate(pair, cosine, minus, plus):
    half = ROT // 2
    return (
        pair * cosine
        + pltpu.roll(pair, LANES - half, 1) * minus
        + pltpu.roll(pair, half, 1) * plus
    )


def unrotate(pair, cosine, minus, plus):
    half = ROT // 2
    return (
        pair * cosine
        - pltpu.roll(pair, LANES - half, 1) * minus
        - pltpu.roll(pair, half, 1) * plus
    )


def normalize(values, gain, shift):
    center = values - jnp.mean(values, axis=-1, keepdims=True)
    spread = jnp.mean(center * center, axis=-1, keepdims=True)
    return center * lax.rsqrt(spread + EPS) * gain + shift


def whole(shape):
    return pl.BlockSpec(
        shape, lambda *idx: (0,) * len(shape), pipeline_mode=pl.Buffered(1)
    )


def held(shape):
    return pl.BlockSpec(shape, lambda *idx: (0,) * len(shape))


def rows_of(tile, width):
    return pl.BlockSpec((tile, width), lambda i, *refs: (i, 0))


def shaped(shape, dtype):
    return jax.ShapeDtypeStruct(shape, dtype)


def params(semantics=1):
    return pltpu.CompilerParams(
        dimension_semantics=("arbitrary",) * semantics, vmem_limit_bytes=VMEM_LIMIT
    )


SUM_ROWS = (2, 4, 16)


class Net:
    def __init__(self):
        dp, mp = lax.axis_index("dp"), lax.axis_index("mp")
        self.half, self.core = mp // 2, lax.rem(mp, 2)
        self.x, self.z = lax.rem(dp, 2), dp // 2
        self.other_half, self.other_core, self.other_x = 1 - self.half, 1 - self.core, 1 - self.x
        self.x_peer = (dp + 1 - 2 * self.x, mp)
        self.y_peer = (dp, mp + 2 - 4 * self.half)
        self.core_peer = (dp, mp + 1 - 2 * self.core)
        self.z_places = [lax.rem(self.z + j, 4) for j in range(1, 4)]
        self.z_peers = [(place * 2 + self.x, mp) for place in self.z_places]
        self.started = []

    def copy(self, src, dst, sems, slot, peer):
        return pltpu.make_async_remote_copy(
            src_ref=src, dst_ref=dst, send_sem=sems.at[0, slot], recv_sem=sems.at[1, slot], device_id=peer,
            device_id_type=MESH,
        )

    def start(self, copies):
        for copy in copies:
            copy.start()
        self.started += copies


def arrive(copies):
    for copy in copies:
        copy.wait_recv()


def added(first, *others):
    total = first.astype(F32)
    for other in others:
        total = total + other.astype(F32)
    return total.astype(BF16)


def sum_scratch(order, size):
    one = (16, size)
    first = {"yxz": ((2, 4), (2, 4)), "xyz": ((2, 4), (2, 4)), "xz": ((4,), (4,)), "zx": ((3, 2), (2,))}[order]
    second = {"yxz": ((4,), (4,)), "xyz": ((4,), (4,)), "xz": ((3,), (1,)), "zx": ((1,), (1,))}[order]
    return [pltpu.VMEM(shape + one, BF16) for shape in (*first, *second, (3,), (2, 2, 4))] + [
        pltpu.SemaphoreType.DMA((2, 12))
    ]


def sum_chunk(net, order, source, scratch):
    got1, work1, got2, work2, got3, full, sems = scratch
    x, z, other_x = net.x, net.z, net.other_x
    own, rows, plane = full.at[0, x, z], full.at[0, x], full.at[0, :, z]

    def to_z(src, dst, slot):
        return [
            net.copy(src(place), dst(j), sems, slot + j, peer)
            for j, (place, peer) in enumerate(zip(net.z_places, net.z_peers))
        ]

    def one(src, dst, slot, peer):
        return [net.copy(src, dst, sems, slot, peer)]

    last = work1 if order == "xz" else work2
    if order != "xyz":
        over_y = one(full.at[0], full.at[1], 9, net.y_peer)
    if order == "zx":
        spread = to_z(lambda place: source.at[:, place], lambda j: got1.at[j], 2)
        cross = one(work1.at[other_x], got2.at[0], 0, net.x_peer)
        back = one(own, own, 8, net.x_peer)
        gather = to_z(lambda place: plane, lambda j: plane, 5)
    else:
        spread = to_z(lambda place: last.at[place], lambda j: got3.at[j], 2)
        gather = to_z(lambda place: own, lambda j: own, 5)
        if order == "yxz":
            first = one(source.at[1], got1, 0, net.y_peer)
            second = one(work1.at[other_x], got2, 1, net.x_peer)
        elif order == "xyz":
            first = one(source.at[:, other_x], got1, 0, net.x_peer)
            second = one(work1.at[1], got2, 1, net.y_peer)
            over_y = one(rows, full.at[1, x], 8, net.y_peer)
            over_x = one(full.at[:, x], full.at[:, x], 9, net.x_peer)
        else:
            first = one(source.at[other_x], got1, 0, net.x_peer)
        if order != "xyz":
            over_x = one(rows, rows, 8, net.x_peer)

    def begin(copies):
        return lambda: net.start(copies)

    def after(copies, work, then):
        def stage():
            arrive(copies)
            if work is not None:
                target, value = work
                target[...] = value()
            if then is not None:
                net.start(then)

        return stage

    if order == "zx":
        mine = (work1, lambda: added(source[:, z], got1[0], got1[1], got1[2]))
        total = (own, lambda: added(work1[x], got2[0]))
        return [
            begin(spread), after(spread, mine, cross), after(cross, total, back), after(back, None, gather),
            after(gather, None, over_y), after(over_y, None, None),
        ]
    total = (own, lambda: added(last[z], got3[0], got3[1], got3[2]))
    if order == "yxz":
        head = [begin(first), after(first, (work1, lambda: added(source[0], got1[...])), second)]
        head.append(after(second, (work2, lambda: added(work1[x], got2[...])), spread))
    elif order == "xyz":
        head = [begin(first), after(first, (work1, lambda: added(source[:, x], got1[...])), second)]
        head.append(after(second, (work2, lambda: added(work1[0], got2[...])), spread))
    else:
        head = [begin(first), after(first, (work1, lambda: added(source[x], got1[...])), spread)]
    one_way, other_way = (over_y, over_x) if order == "xyz" else (over_x, over_y)
    return head + [
        after(spread, total, gather), after(gather, None, one_way), after(one_way, None, other_way),
        after(other_way, None, None),
    ]


def sum_both(net, parts, both, got, total, core_sems, scratches):
    exchange = [net.copy(both.at[net.other_core], got, core_sems, 0, net.core_peer)]
    chunks, start = [], 0
    for (order, size), scratch in zip(parts, scratches):
        chunks.append(sum_chunk(net, order, total.at[:, :, :, :, pl.ds(start, size)], scratch))
        start += size

    def combine():
        arrive(exchange)
        for place, at in ((0, net.half), (1, net.other_half)):
            total[place] = added(both[net.core, at], got[at])
        for chunk in chunks:
            chunk[0]()

    def together(k):
        def stage():
            for chunk in chunks:
                if k < len(chunk):
                    chunk[k]()

        return stage

    longest = max(len(chunk) for chunk in chunks)
    return [lambda: net.start(exchange), combine] + [together(k) for k in range(1, longest)]


def both_scratch(parts):
    size = sum(part[1] for part in parts)
    return [
        pltpu.VMEM((2,) + SUM_ROWS + (size,), BF16),
        pltpu.VMEM((2,) + SUM_ROWS + (size,), BF16),
        pltpu.SemaphoreType.DMA((2, 1)),
    ] + [shape for part in parts for shape in sum_scratch(*part)]


def split_columns(size):
    count = (size // 2 + LANES - 1) // LANES * LANES
    return (("yxz", count), ("xyz", size - count))


def quarters(ref, *arrays):
    start = 0
    for array in arrays:
        size = array.shape[1] // 4
        for q in range(4):
            ref[q % 2, q // 2, :, start : start + size] = array[:, q * size : (q + 1) * size].astype(BF16)
        start += size


def gelu_parts(hidden):
    cdf = 0.5 + 0.5 * lax.erf(hidden * math.sqrt(0.5))
    density = jnp.exp(-0.5 * hidden * hidden) * (1.0 / math.sqrt(2.0 * math.pi))
    return hidden * cdf, cdf + hidden * density


def feed_core(rows, grads, up_ref, down_ref, act_ref, grad_ref, hidden_step):
    for start in range(0, up_ref.shape[1], hidden_step):
        cols = pl.ds(start, hidden_step)
        hidden = dot_nn(rows, up_ref[:, cols])
        grad_act = dot_nt(grads, down_ref[cols, :])
        activated, slope = gelu_parts(hidden)
        act_ref[:, cols] = activated.astype(BF16)
        grad_ref[:, cols] = (grad_act * slope).astype(BF16)


def shard_index(unit, far):
    return lax.rem(lax.axis_index("mp") + (unit if far else 0), 2 * unit)


def columns_of(ref, size, shard):
    return ref.at[:, pl.ds(pl.multiple_of(shard * size, size), size)]


def rows_at(ref, size, shard):
    return ref.at[pl.ds(pl.multiple_of(shard * size, size), size)]


def load(step, sems, pairs):
    copies = [pltpu.make_async_copy(src, dst, sems.at[j]) for j, (src, dst) in enumerate(pairs)]

    @pl.when(step == 0)
    def _():
        for copy in copies:
            copy.start()
        for copy in copies:
            copy.wait()


def head_weights(unit, triples, right, outputs, output_left, triple_ref, output_ref):
    width = triples[0].shape[0]
    head_width = outputs[0].shape[0]
    size = 3 * head_width
    pairs = []
    for j in range(2):
        shard = shard_index(unit, j == 1)
        cols, rows = pl.ds(j * size, size), pl.ds(j * head_width, head_width)
        pairs += [
            (triples[j], triple_ref.at[pl.ds(0, width), cols]),
            (columns_of(right, size, shard), triple_ref.at[pl.ds(width, LANES), cols]),
            (outputs[j], output_ref.at[rows, pl.ds(0, width)]),
            (rows_at(output_left, head_width, shard), output_ref.at[rows, pl.ds(width, LANES)]),
        ]
    return pairs


def chip_neighbours(unit):
    dp = lax.axis_index("dp")
    mp = lax.axis_index("mp")
    lead = lax.rem(dp, 2)
    return lead, (dp, lax.rem(mp + unit, 2 * unit)), (dp + 1 - 2 * lead, mp)


def leads():
    dp = lax.axis_index("dp")
    return lax.rem(dp, 2), lax.rem(dp // 2, 2)


def courier(unit, pairs, chunks, y_sems, x_sems):
    lead, y_peer, x_peer = chip_neighbours(unit)
    over_y, over_x = [], []
    for k in range(chunks):
        for j, (own, far) in enumerate(pairs):
            count = own.shape[0] // 2 // chunks
            span = pl.ds(pl.multiple_of((lead * chunks + k) * count, count), count)
            for src, sems, peer, group in ((own, y_sems, y_peer, over_y), (far, x_sems, x_peer, over_x)):
                group.append(
                    pltpu.make_async_remote_copy(
                        src_ref=src.at[span],
                        dst_ref=far.at[span],
                        send_sem=sems.at[0, k, j],
                        recv_sem=sems.at[1, k, j],
                        device_id=peer,
                        device_id_type=MESH,
                    )
                )
    return over_y, over_x


def meet(peers):
    barrier = pltpu.get_barrier_semaphore()
    for peer in peers:
        pl.semaphore_signal(barrier, inc=1, device_id=peer, device_id_type=MESH)
    pl.semaphore_wait(barrier, len(peers))


def place_in_unit(unit):
    mp = lax.axis_index("mp")
    return lax.rem(mp, unit), mp - lax.rem(mp, unit)


def unit_peers(unit):
    place, base = place_in_unit(unit)
    return [(lax.axis_index("dp"), base + lax.rem(place + unit - s, unit)) for s in range(1, unit)]


def halo_copies(unit, x_ref, halo_ref, y_sems, unit_sems):
    own_rows = x_ref.shape[0]
    chunk = math.gcd(own_rows, 128)
    dp = lax.axis_index("dp")
    found = []
    for k in range(SHORT // chunk):
        row = unit * own_rows - SHORT + k * chunk
        holder, start = row // own_rows, row % own_rows
        target = halo_ref.at[pl.ds(k * chunk, chunk)]
        over_y = pltpu.make_async_remote_copy(
            src_ref=x_ref.at[pl.ds(start, chunk)], dst_ref=target, send_sem=y_sems.at[0, k], recv_sem=y_sems.at[1, k],
            device_id=(dp, unit + holder), device_id_type=MESH,
        )
        spread = [
            pltpu.make_async_remote_copy(
                src_ref=target, dst_ref=target, send_sem=unit_sems.at[0, k, s - 1], recv_sem=unit_sems.at[1, k, s - 1],
                device_id=(dp, unit + (holder + s) % unit), device_id_type=MESH,
            )
            for s in range(1, unit)
        ]
        found.append((holder, over_y, spread))
    return found


def feed_first_kernel(
    unit, tile, x_ref, dy_ref, gain1_ref, shift1_ref, gain2_ref, shift2_ref, up_own_ref, up_left_ref, up_right_ref,
    down_own_ref, down_left_ref, output_right_ref, down_right_ref, x_all_ref, dy_all_ref, triple_ref, output_ref, normed1_ref,
    normed_ref, dy_full_ref, low_ref, grad_lows_ref, out_ref, grad_ref, low_act_ref, grad_low_ref, sums_ref,
    triple_far_ref, output_far_ref, halo_ref, up_half_ref, down_half_ref, act_ref, gh_ref, up_ref, down_ref, acc_ref,
    xs_ref, x_got_ref, dy_got_ref, y_sems, x_sems, unit_sems, halo_y_sems, halo_unit_sems, local_sems, load_sems,
):
    step = pl.program_id(0)
    width, hidden = up_own_ref.shape
    weights = (
        (up_own_ref, up_ref.at[pl.ds(0, width)]),
        (columns_of(up_right_ref, hidden, shard_index(unit, False)), up_ref.at[pl.ds(width, LANES)]),
        (down_own_ref, down_ref.at[:, pl.ds(0, width)]),
        (rows_at(down_left_ref, hidden, shard_index(unit, False)), down_ref.at[:, pl.ds(width, LANES)]),
    )
    own_rows = x_all_ref.shape[0]
    per_device = own_rows // tile
    steps = unit * per_device
    chunks = y_sems.shape[1]
    place, base = place_in_unit(unit)
    half = base // unit
    peers = unit_peers(unit)
    over_y, over_x = courier(
        unit, ((triple_ref, triple_far_ref), (output_ref, output_far_ref)), chunks, y_sems, x_sems
    )
    halo = halo_copies(unit, x_all_ref, halo_ref, halo_y_sems, halo_unit_sems)
    rows_out = [
        pltpu.make_async_remote_copy(
            src_ref=src, dst_ref=dst.at[j], send_sem=unit_sems.at[0, which, j], recv_sem=unit_sems.at[1, which, j],
            device_id=peer, device_id_type=MESH,
        )
        for j, peer in enumerate(peers)
        for which, (src, dst) in enumerate(((x_all_ref, x_got_ref), (dy_all_ref, dy_got_ref)))
    ]
    kept_halves = [
        pltpu.make_async_copy(
            src.at[
                pl.ds(pl.multiple_of(lead * dst.shape[0], dst.shape[0]), dst.shape[0]), pl.ds(0, dst.shape[1])
            ],
            dst,
            local_sems.at[j],
        )
        for j, (lead, src, dst) in enumerate(zip(leads(), (up_ref, down_ref), (up_half_ref, down_half_ref)))
    ]

    @pl.when(step == 0)
    def _():
        meet([*chip_neighbours(unit)[1:], *peers])
        for copy in rows_out + over_y:
            copy.start()

    for holder, copy, _ in halo:
        pl.when((step == 0) & (half == 0) & (place == holder))(copy.start)
    load(step, load_sems, weights)

    @pl.when(step == 0)
    def _():
        for copy in kept_halves:
            copy.start()
        xs_ref[...] = x_ref[...]
        dy_full_ref[...] = dy_ref[...]

    @pl.when((step > 0) & (step < per_device))
    def _():
        xs_ref[...] = x_ref[...]
        dy_full_ref[...] = dy_ref[...]

    for slot in range(unit - 1):

        @pl.when(step == per_device * (slot + 1))
        def _():
            for which in range(2):
                rows_out[2 * slot + which].wait_recv()

        @pl.when((step >= per_device * (slot + 1)) & (step < per_device * (slot + 2)))
        def _():
            span = pl.ds(pl.multiple_of((step - per_device * (slot + 1)) * tile, tile), tile)
            xs_ref[...] = x_got_ref[slot, span]
            dy_full_ref[...] = dy_got_ref[slot, span]

    for k in range(chunks):

        @pl.when(step == min(k + 1, steps - 1))
        def _():
            for j in (2 * k, 2 * k + 1):
                over_y[j].wait_recv()
                over_x[j].start()

    x = xs_ref[...].astype(F32)
    center = x - jnp.mean(x, axis=-1, keepdims=True)
    spread = jnp.mean(center * center, axis=-1, keepdims=True)
    scaled = center * lax.rsqrt(spread + EPS)
    normed1_ref[...] = (scaled * gain1_ref[...] + shift1_ref[...]).astype(BF16)
    normed = (scaled * gain2_ref[...] + shift2_ref[...]).astype(BF16)
    normed_ref[...] = normed
    dy = dy_full_ref[...]
    low = dot_nn(normed, up_left_ref[...]).astype(BF16)
    low_ref[...] = low
    rights = jnp.concatenate([output_right_ref[...], down_right_ref[...]], axis=0)
    grad_lows = dot_nt(dy, rights).astype(BF16)
    grad_lows_ref[...] = grad_lows
    grad_low = grad_lows[:, LANES:]
    feed_core(
        jnp.concatenate([normed, low], axis=1), jnp.concatenate([dy, grad_low], axis=1), up_ref, down_ref, act_ref,
        gh_ref, 512,
    )
    act = act_ref[...]
    gh = gh_ref[...]
    forward = dot_nn(act, down_ref[...])
    backward = dot_nt(gh, up_ref[...])
    out_ref[...], low_act_ref[...] = forward[:, :width], forward[:, width:]
    grad_ref[...], grad_low_ref[...] = backward[:, :width], backward[:, width:]

    @pl.when(step == 0)
    def _():
        acc_ref[...] = jnp.zeros_like(acc_ref)

    acc_ref[:, :hidden] += dot_tn(low, gh)
    acc_ref[:, hidden:] += dot_tn(grad_low, act)

    @pl.when((step == 0) & (half == 0))
    def _():
        fills = [
            pltpu.make_async_copy(xs_ref, halo_ref.at[pl.ds(k * tile, tile)], local_sems.at[2 + k])
            for k in range(SHORT // tile)
        ]
        for copy in fills:
            copy.start()
        for copy in fills:
            copy.wait()

    @pl.when(step == steps - 1)
    def _():
        sums_ref[...] = acc_ref[...].astype(BF16)
        for holder, copy, spread_copies in halo:

            @pl.when((half == 1) & (place == holder))
            def _():
                copy.wait_recv()
                for other in spread_copies:
                    other.start()

        for holder, copy, spread_copies in halo:
            pl.when((half == 0) & (place == holder))(copy.wait_send)

            @pl.when((half == 1) & (place == holder))
            def _():
                for other in spread_copies:
                    other.wait_send()

            for s in range(1, unit):
                pl.when((half == 1) & (place == (holder + s) % unit))(spread_copies[s - 1].wait_recv)
        for copy in rows_out + over_y:
            copy.wait_send()
        for copy in over_x + kept_halves:
            copy.wait()


def feed_first(unit, x, dy, norms, up, up_left, up_right, down, down_left, output_right, down_right, triple, output,
               tile):
    own_rows, width = x.shape
    rows = own_rows * unit
    hidden = up.shape[1]
    steps, per_device = rows // tile, own_rows // tile
    chunks = math.gcd(4, output.shape[0] // 32)
    halo_chunks = SHORT // math.gcd(own_rows, 128)
    anywhere = pl.BlockSpec(memory_space=pl.ANY)
    here = pl.BlockSpec((tile, width), lambda i: (jnp.minimum(i, per_device - 1), 0))

    def turned(size):
        def index(i):
            return (lax.rem(i + place_in_unit(unit)[0] * per_device, steps), 0)

        return pl.BlockSpec((tile, size), index)

    return pl.pallas_call(
        functools.partial(feed_first_kernel, unit, tile),
        grid=(steps,),
        in_specs=[here, here]
        + [whole((1, width))] * 4
        + [
            anywhere,
            whole(up_left.shape),
            anywhere,
            anywhere,
            anywhere,
            whole(output_right.shape),
            whole(down_right.shape),
        ]
        + [anywhere] * 4,
        out_specs=[
            turned(width),
            turned(width),
            turned(width),
            turned(LANES),
            turned(2 * LANES),
            turned(width),
            turned(width),
            turned(LANES),
            turned(LANES),
            held((LANES, 2 * hidden)),
        ]
        + [anywhere] * 5,
        scratch_shapes=[
            pltpu.VMEM((tile, hidden), BF16),
            pltpu.VMEM((tile, hidden), BF16),
            pltpu.VMEM((width + LANES, hidden), BF16),
            pltpu.VMEM((hidden, width + LANES), BF16),
            pltpu.VMEM((LANES, 2 * hidden), F32),
            pltpu.VMEM((tile, width), BF16),
            pltpu.VMEM((unit - 1, own_rows, width), BF16),
            pltpu.VMEM((unit - 1, own_rows, width), BF16),
            pltpu.SemaphoreType.DMA((2, chunks, 2)),
            pltpu.SemaphoreType.DMA((2, chunks, 2)),
            pltpu.SemaphoreType.DMA((2, 2, unit - 1)),
            pltpu.SemaphoreType.DMA((2, halo_chunks)),
            pltpu.SemaphoreType.DMA((2, halo_chunks, unit - 1)),
            pltpu.SemaphoreType.DMA((2 + SHORT // tile,)),
            pltpu.SemaphoreType.DMA((4,)),
        ],
        out_shape=[
            shaped((rows, width), BF16),
            shaped((rows, width), BF16),
            shaped((rows, width), BF16),
            shaped((rows, LANES), BF16),
            shaped((rows, 2 * LANES), BF16),
            shaped((rows, width), F32),
            shaped((rows, width), F32),
            shaped((rows, LANES), F32),
            shaped((rows, LANES), F32),
            shaped((LANES, 2 * hidden), BF16),
            shaped(triple.shape, BF16),
            shaped(output.shape, BF16),
            shaped((SHORT, width), BF16),
            shaped((up.shape[0] // 2, up.shape[1]), BF16),
            shaped((down.shape[0] // 2, down.shape[1]), BF16),
        ],
        compiler_params=pltpu.CompilerParams(
            dimension_semantics=("arbitrary",), vmem_limit_bytes=VMEM_LIMIT, collective_id=3, has_side_effects=True
        ),
        cost_estimate=BRIEF,
        name="feed_first",
    )(x, dy, *norms, up, up_left, up_right, down, down_left, output_right, down_right, x, dy, triple, output)


def feed_second_kernel(
    unit, tile, normed_ref, low_ref, dy_ref, grad_lows_ref, out_in_ref, grad_in_ref, low_act_in_ref, grad_low_in_ref,
    x_ref, keep_ref, got1_ref, gain1_ref, gain2_ref, output_right_ref, down_right_ref, up0_ref, up1_ref, up_left_ref,
    up_right_ref, down0_ref, down1_ref, down_left_ref, early_ref, heads_ref, left_ref, y_ref, dx_ref, sums_ref, both_ref,
    heads_out_ref, left_out_ref, act_ref, gh_ref, up_ref, down_ref, send_ref, got_ref, early_got_ref, acc_ref, norms_ref,
    output_right_grad_ref, down_right_grad_ref, up_left_grad_ref, sems, early_sems, out_sems, load_sems, *sum_refs,
):
    step = pl.program_id(0)
    own_rows = got_ref.shape[1]
    per_device = own_rows // tile
    send_tiles = (unit - 1) * per_device
    width, hidden = up_ref.shape[0] - LANES, up_ref.shape[1]
    shard = shard_index(unit, True)
    weights = [
        (columns_of(up_right_ref, hidden, shard), up_ref.at[pl.ds(width, LANES)]),
        (rows_at(down_left_ref, hidden, shard), down_ref.at[:, pl.ds(width, LANES)]),
    ]
    for lead, pieces, ref in zip(leads(), ((up0_ref, up1_ref), (down0_ref, down1_ref)), (up_ref, down_ref)):
        for place, piece in zip((lead, 1 - lead), pieces):
            weights.append((piece, rows_at(ref, piece.shape[0], place).at[:, pl.ds(0, piece.shape[1])]))
    peers = unit_peers(unit)
    copies = [
        [
            pltpu.make_async_remote_copy(
                src_ref=send_ref.at[s, pl.ds(t * tile, tile)], dst_ref=got_ref.at[s, pl.ds(t * tile, tile)],
                send_sem=sems.at[0, s, t], recv_sem=sems.at[1, s, t], device_id=peer, device_id_type=MESH,
            )
            for t in range(per_device)
        ]
        for s, peer in enumerate(peers)
    ]

    steps = unit * per_device
    y_peer = chip_neighbours(unit)[1]
    pieces = early_sems.shape[1]
    count = early_ref.shape[0] // pieces
    early_copies = [
        pltpu.make_async_remote_copy(
            src_ref=early_ref.at[pl.ds(j * count, count)], dst_ref=early_got_ref.at[pl.ds(j * count, count)],
            send_sem=early_sems.at[0, j], recv_sem=early_sems.at[1, j], device_id=y_peer, device_id_type=MESH,
        )
        for j in range(pieces)
    ]
    hosted = len(sum_refs) > 0
    if hosted:
        net = Net()
        size = heads_ref.shape[-1] // 2
        split = len(sum_scratch("yxz", size))
        heads_refs = (sum_refs[:split], sum_refs[split : 2 * split])
        left_refs = sum_refs[2 * split :]
        stages = [
            sum_chunk(net, order, heads_ref.at[:, :, :, :, pl.ds(j * size, size)], heads_refs[j])
            for j, order in enumerate(("yxz", "xyz"))
        ]
        stages.append(sum_both(net, (("yxz", left_ref.shape[-1]),), left_ref, *left_refs[:3], (left_refs[3:],)))

    def advance():
        if hosted:
            for at in range(steps):

                @pl.when(step == at)
                def _():
                    for stage in stages:
                        stage[at]()

    @pl.when(step == 0)
    def _():
        meet([*peers, y_peer] + ([net.x_peer, *net.z_peers] if hosted else []))
        for ref in (norms_ref, output_right_grad_ref, down_right_grad_ref, acc_ref, up_left_grad_ref):
            ref[...] = jnp.zeros_like(ref)

    advance()
    for j, copy in enumerate(early_copies):
        pl.when(step == min(j + 1, steps - 1))(copy.start)
    load(step, load_sems, weights)
    normed = normed_ref[...]
    low = low_ref[...]
    dy = dy_ref[...]
    grad_low = grad_lows_ref[:, LANES:]
    feed_core(
        jnp.concatenate([normed, low], axis=1), jnp.concatenate([dy, grad_low], axis=1), up_ref, down_ref, act_ref,
        gh_ref, 512,
    )
    act = act_ref[...]
    gh = gh_ref[...]
    forward = dot_nn(act, down_ref[...])
    backward = dot_nt(gh, up_ref[...])
    grad_low_up = (grad_low_in_ref[...] + backward[:, width:]).astype(BF16)
    out = out_in_ref[...] + forward[:, :width]
    low_act = low_act_in_ref[...] + forward[:, width:]
    second = grad_in_ref[...] + backward[:, :width] + dot_nt(grad_low_up, up_left_ref[...])
    acc_ref[:, :hidden] += dot_tn(low, gh)
    acc_ref[:, hidden:] += dot_tn(grad_low, act)
    up_left_grad_ref[...] += dot_tn(grad_low_up, normed)

    @pl.when(step < send_tiles)
    def _():
        slot = step // per_device
        span = pl.ds(pl.multiple_of(lax.rem(step, per_device) * tile, tile), tile)
        send_ref[slot, span, :width] = out.astype(BF16)
        send_ref[slot, span, width : 2 * width] = second.astype(BF16)
        send_ref[slot, span, 2 * width :] = low_act.astype(BF16)

    for s in range(unit - 1):
        for t in range(per_device):
            pl.when(step == s * per_device + t)(copies[s][t].start)
            pl.when(step == send_tiles + t)(copies[s][t].wait_recv)

    @pl.when(step >= send_tiles)
    def _():
        span = pl.ds(pl.multiple_of((step - send_tiles) * tile, tile), tile)
        first = keep_ref[:, :width].astype(F32)
        low_att = keep_ref[:, width:].astype(F32)
        total_out, total_second, total_low = out, second, low_act
        for s in range(unit - 1):
            first = first + got1_ref[s, :, :width].astype(F32)
            low_att = low_att + got1_ref[s, :, width:].astype(F32)
            total_out = total_out + got_ref[s, span, :width].astype(F32)
            total_second = total_second + got_ref[s, span, width : 2 * width].astype(F32)
            total_low = total_low + got_ref[s, span, 2 * width :].astype(F32)
        low_att, total_low = low_att.astype(BF16), total_low.astype(BF16)
        x = x_ref[...].astype(F32)
        y_ref[...] = (
            x + total_out + dot_nn(low_att, output_right_ref[...]) + dot_nn(total_low, down_right_ref[...])
        ).astype(BF16)
        center = x - jnp.mean(x, axis=-1, keepdims=True)
        spread = jnp.mean(center * center, axis=-1, keepdims=True)
        inverse = lax.rsqrt(spread + EPS)
        scaled = center * inverse
        total = first * gain1_ref[...] + total_second * gain2_ref[...]
        mean = jnp.mean(total, axis=-1, keepdims=True)
        inner = jnp.mean(total * scaled, axis=-1, keepdims=True)
        dx_ref[...] = dy.astype(F32) + (total - mean - scaled * inner) * inverse
        norms_ref[0:1, :] += jnp.sum(first * scaled, axis=0, keepdims=True)
        norms_ref[1:2, :] += jnp.sum(first, axis=0, keepdims=True)
        norms_ref[2:3, :] += jnp.sum(total_second * scaled, axis=0, keepdims=True)
        norms_ref[3:4, :] += jnp.sum(total_second, axis=0, keepdims=True)
        output_right_grad_ref[...] += dot_tn(low_att, dy)
        down_right_grad_ref[...] += dot_tn(total_low, dy)

    @pl.when(step == steps - 1)
    def _():
        for copy in early_copies:
            copy.wait()
        sums_ref[...] = (acc_ref[...] + early_got_ref[...].astype(F32)).astype(BF16)
        quarters(both_ref, up_left_grad_ref[...], output_right_grad_ref[...], down_right_grad_ref[...])
        start = 3 * (width // 4)
        count = width // LANES
        for q in range(4):
            rows = [norms_ref[q : q + 1, j * LANES : (j + 1) * LANES] for j in range(count)]
            block = jnp.concatenate([*rows, jnp.zeros((LANES - count, LANES), F32)], axis=0)
            both_ref[q % 2, q // 2, :, start:] = block.astype(BF16)
        for group in copies:
            for copy in group:
                copy.wait_send()
        if hosted:
            for at in range(steps, max(len(stage) for stage in stages)):
                for stage in stages:
                    if at < len(stage):
                        stage[at]()
            outs = []
            for j, refs in enumerate((*heads_refs, left_refs[3:])):
                full = refs[5]
                target = left_out_ref if j == 2 else heads_out_ref.at[:, :, :, :, pl.ds(j * size, size)]
                outs.append(pltpu.make_async_copy(full, target, out_sems.at[j]))
                outs[-1].start()
            for copy in net.started:
                copy.wait_send()
            for copy in outs:
                copy.wait()


def feed_second(unit, normed, low, dy, grad_lows, out, grad, low_act, grad_low, x, keep, got, gains, output_right,
                down_right, ups, up_left, up_right, downs, down_left, early, heads, left, hosted, tile):
    rows, width = normed.shape
    own_rows = rows // unit
    anywhere = pl.BlockSpec(memory_space=pl.ANY)
    extra = []
    if hosted:
        heads = heads.reshape((2,) + SUM_ROWS + heads.shape[-1:])
        left = left.reshape((2, 2) + SUM_ROWS + left.shape[-1:])
        extra = sum_scratch("yxz", heads.shape[-1] // 2) + sum_scratch("xyz", heads.shape[-1] // 2)
        extra += both_scratch((("yxz", left.shape[-1]),))
    hidden = ups[0].shape[1]
    steps, per_device = rows // tile, own_rows // tile
    send_tiles = steps - per_device
    wide = 2 * width + LANES

    def turned(size):
        def index(i):
            place, slot = place_in_unit(unit)[0], i // per_device + 1
            return (lax.rem(place + unit - slot, unit) * per_device + lax.rem(i, per_device), 0)

        return pl.BlockSpec((tile, size), index)

    def late(size):
        return pl.BlockSpec((tile, size), lambda i: (jnp.maximum(i - send_tiles, 0), 0))

    return pl.pallas_call(
        functools.partial(feed_second_kernel, unit, tile),
        grid=(steps,),
        in_specs=[
            turned(width),
            turned(LANES),
            turned(width),
            turned(2 * LANES),
            turned(width),
            turned(width),
            turned(LANES),
            turned(LANES),
            late(width),
            late(width + LANES),
            pl.BlockSpec((unit - 1, tile, width + LANES), lambda i: (0, jnp.maximum(i - send_tiles, 0), 0)),
            whole((1, width)),
            whole((1, width)),
            whole(output_right.shape),
            whole(down_right.shape),
            anywhere,
            anywhere,
            whole(up_left.shape),
            anywhere,
            anywhere,
            anywhere,
            anywhere,
            whole(early.shape),
            whole(heads.shape),
            whole(left.shape),
        ],
        out_specs=[
            late(width),
            late(width),
            held((LANES, 2 * hidden)),
            held((2, 2, LANES, 3 * (width // 4) + LANES)),
            anywhere,
            anywhere,
        ],
        scratch_shapes=[
            pltpu.VMEM((tile, hidden), BF16),
            pltpu.VMEM((tile, hidden), BF16),
            pltpu.VMEM((width + LANES, hidden), BF16),
            pltpu.VMEM((hidden, width + LANES), BF16),
            pltpu.VMEM((unit - 1, own_rows, wide), BF16),
            pltpu.VMEM((unit - 1, own_rows, wide), BF16),
            pltpu.VMEM((LANES, 2 * hidden), BF16),
            pltpu.VMEM((LANES, 2 * hidden), F32),
            pltpu.VMEM((8, width), F32),
            pltpu.VMEM((LANES, width), F32),
            pltpu.VMEM((LANES, width), F32),
            pltpu.VMEM((LANES, width), F32),
            pltpu.SemaphoreType.DMA((2, unit - 1, per_device)),
            pltpu.SemaphoreType.DMA((2, 4)),
            pltpu.SemaphoreType.DMA((3,)),
            pltpu.SemaphoreType.DMA((6,)),
        ]
        + extra,
        out_shape=[
            shaped((own_rows, width), BF16),
            shaped((own_rows, width), F32),
            shaped((LANES, 2 * hidden), BF16),
            shaped((2, 2, LANES, 3 * (width // 4) + LANES), BF16),
            shaped(heads.shape, BF16),
            shaped(left.shape[1:] if hosted else left.shape, BF16),
        ],
        compiler_params=pltpu.CompilerParams(
            dimension_semantics=("arbitrary",), vmem_limit_bytes=VMEM_LIMIT, collective_id=4, has_side_effects=True
        ),
        cost_estimate=BRIEF,
        name="feed_second",
    )(normed, low, dy, grad_lows, out, grad, low_act, grad_low, x, keep, got, *gains, output_right, down_right, *ups,
      up_left, up_right, *downs, down_left, early, heads, left)


def project_kernel(
    unit, main_tiles, halo_ref, normed_ref, dy_ref, grad_lows_ref, late_ref, cos0_ref, cos1_ref, minus0_ref, minus1_ref, plus0_ref,
    plus1_ref, gain_ref, shift_ref, triple0_ref, triple1_ref, left_ref, right_ref, output0_ref, output1_ref,
    output_left_ref, low_ref, q_ref, k_ref, v_ref, g_ref, triple_ref, output_ref, load_sems,
):
    step = pl.program_id(0)
    load(
        step, load_sems,
        head_weights(
            unit, (triple0_ref, triple1_ref), right_ref, (output0_ref, output1_ref), output_left_ref, triple_ref,
            output_ref,
        ),
    )

    later = late_ref[0, 0:1, :] > 0.0
    tables = tuple(
        jnp.where(later, two[...], one[...])
        for one, two in ((cos0_ref, cos1_ref), (minus0_ref, minus1_ref), (plus0_ref, plus1_ref))
    )
    head_width = output0_ref.shape[0]
    first = low_lanes()

    def rows(normed, full):
        low = dot_nn(normed, left_ref[...]).astype(BF16)
        if full:
            low_ref[...] = low
        mixed = dot_nn(jnp.concatenate([normed, low], axis=1), triple_ref[...])
        if full:
            grads = jnp.concatenate([dy_ref[...], grad_lows_ref[:, :LANES]], axis=1)
            g_ref[...] = dot_nt(grads, output_ref[...]).astype(BF16)
        for pair in range(2 * head_width // LANES):
            one, two, three = (
                mixed[:, (3 * pair + part) * LANES : (3 * pair + part + 1) * LANES] for part in range(3)
            )
            cols = pl.ds(pair * LANES, LANES)
            key = pltpu.roll(jnp.where(first, three, one), HEAD_DIM, 1)
            k_ref[:, cols] = rotate(key, *tables).astype(BF16)
            v_ref[:, cols] = jnp.where(first, two, three).astype(BF16)
            if full:
                query = rotate(jnp.where(first, one, two), *tables).astype(BF16)
                q_ref[:, cols] = query * HEAD_DIM**-0.5

    @pl.when(step < main_tiles)
    def _():
        rows(normed_ref[...], True)

    @pl.when(step >= main_tiles)
    def _():
        rows(normalize(halo_ref[...].astype(F32), gain_ref[...], shift_ref[...]).astype(BF16), False)


def project(unit, conts, x_halo, normed, dy, grad_lows, gain, shift, triples, left, right, outputs, output_left, tables,
            tile):
    rows, width = dy.shape
    head_width = outputs[0].shape[0]
    anywhere = pl.BlockSpec(memory_space=pl.ANY)
    per_block = SHORT // tile
    main_tiles, halo_tiles = rows // tile, SHORT // tile
    late = jnp.concatenate([jnp.repeat(conts, per_block), jnp.zeros((halo_tiles,), jnp.int32)])
    late = jnp.broadcast_to(late.astype(F32)[:, None, None], (main_tiles + halo_tiles, 8, LANES))

    halo = pl.BlockSpec((tile, width), lambda i: (jnp.maximum(i - main_tiles, 0), 0))

    def table(which):
        return pl.BlockSpec((tile, LANES), lambda i: (which * per_block + lax.rem(i, per_block), 0))

    def main(size):
        return pl.BlockSpec((tile, size), lambda i: (jnp.minimum(i, main_tiles - 1), 0))

    def all_rows(size):
        return pl.BlockSpec((tile, size), lambda i: (jnp.where(i < main_tiles, i + halo_tiles, i - main_tiles), 0))

    return pl.pallas_call(
        functools.partial(project_kernel, unit, main_tiles),
        grid=(main_tiles + halo_tiles,),
        in_specs=[
            halo,
            main(width),
            main(width),
            main(2 * LANES),
            pl.BlockSpec((1, 8, LANES), lambda i: (i, 0, 0)),
            table(0),
            table(1),
            table(0),
            table(1),
            table(0),
            table(1),
            whole(gain.shape),
            whole(shift.shape),
            anywhere,
            anywhere,
            whole(left.shape),
            anywhere,
            anywhere,
            anywhere,
            anywhere,
        ],
        out_specs=[
            main(LANES),
            main(2 * head_width),
            all_rows(2 * head_width),
            all_rows(2 * head_width),
            main(2 * head_width),
        ],
        scratch_shapes=[
            pltpu.VMEM((width + LANES, 6 * head_width), BF16),
            pltpu.VMEM((2 * head_width, width + LANES), BF16),
            pltpu.SemaphoreType.DMA((8,)),
        ],
        out_shape=[
            shaped((rows, LANES), BF16),
            shaped((rows, 2 * head_width), BF16),
            shaped((SHORT + rows, 2 * head_width), BF16),
            shaped((SHORT + rows, 2 * head_width), BF16),
            shaped((rows, 2 * head_width), BF16),
        ],
        compiler_params=params(),
        cost_estimate=BRIEF,
        name="project",
    )(x_halo, normed, dy, grad_lows, late, *[table for table in tables for _ in range(2)], gain, shift, *triples, left, right,
      *outputs, output_left)


def attend_rows(with_prev, pairs, count, allowed, q_ref, k_ref, v_ref, g_ref, kp_ref, vp_ref, tables, att_ref, gq_ref,
                dk_ref, dv_ref, dkp_ref, dvp_ref):
    first = low_lanes()
    zero = jnp.zeros((), BF16)

    def stack(pair):
        return jnp.concatenate([jnp.where(first, pair, zero), jnp.where(first, zero, pair)], axis=0)

    def unstack(both):
        return jnp.where(first, both[:count], both[count:])

    def joined(fold, values):
        return functools.reduce(fold, values)

    pieces = []
    for lanes in pairs:
        for start in range(0, SHORT, count):
            span = pl.ds(start, count)
            parts = []
            if with_prev:
                parts.append((kp_ref[:, lanes], vp_ref[:, lanes], dkp_ref, dvp_ref, pl.ds(0, SHORT)))
            if start:
                before = pl.ds(0, start)
                parts.append((k_ref[before, lanes], v_ref[before, lanes], dk_ref, dv_ref, before))
            parts.append((k_ref[span, lanes], v_ref[span, lanes], dk_ref, dv_ref, span))
            pieces.append((lanes, span, stack(q_ref[span, lanes]), stack(g_ref[span, lanes]), parts))

    scores, grads, weights, lows, inners, slopes = [], [], [], [], [], []
    for _, _, queries, _, parts in pieces:
        found = [dot_nt(queries, part[0]) for part in parts]
        scores.append(found[:-1] + [jnp.where(allowed, found[-1], -1e30)])
    for _, _, _, grad, parts in pieces:
        grads.append([dot_nt(grad, part[1]) for part in parts])
    for found in scores:
        peak = joined(jnp.maximum, [jnp.max(score, axis=1, keepdims=True) for score in found])
        exps = [jnp.exp(score - peak) for score in found]
        scale = 1.0 / joined(jnp.add, [jnp.sum(exp, axis=1, keepdims=True) for exp in exps])
        weights.append([exp * scale for exp in exps])
        lows.append([weight.astype(BF16) for weight in weights[-1]])
    for (lanes, span, _, grad, parts), low in zip(pieces, lows):
        attended = joined(jnp.add, [dot_nn(weight, part[1]) for weight, part in zip(low, parts)])
        att_ref[span, lanes] = unstack(attended).astype(BF16)
        inners.append(jnp.sum(attended * grad.astype(F32), axis=1, keepdims=True))
    for weight, grad, inner in zip(weights, grads, inners):
        slopes.append([(w * (g - inner)).astype(BF16) for w, g in zip(weight, grad)])
    for (lanes, span, queries, grad, parts), low, slope in zip(pieces, lows, slopes):
        grad_query = joined(jnp.add, [dot_nn(ds, part[0]) for ds, part in zip(slope, parts)])
        for ds, weight, (_, _, to_key, to_value, rows) in zip(slope, low, parts):
            to_key[lanes, rows] += dot_tn(queries, ds)
            to_value[lanes, rows] += dot_tn(grad, weight)
        grad_query = unstack(grad_query) * HEAD_DIM**-0.5
        gq_ref[span, lanes] = unrotate(grad_query, *[table[span] for table in tables]).astype(BF16)


def unrotate_tall(ref, lanes, cosine, sine):
    half = ROT // 2
    value = ref[lanes, :]
    halves = []
    for base in (HEAD_DIM, 0):
        one, two = value[base : base + half], value[base + half : base + ROT]
        halves += [one * cosine + two * sine, two * cosine - one * sine, value[base + ROT : base + HEAD_DIM]]
    return jnp.concatenate(halves, axis=0).astype(BF16).T


def attend_kernel(
    blocks, pairs, count, conts_ref, q_ref, k_ref, v_ref, g_ref, kp_ref, vp_ref, cos_ref, minus_ref, plus_ref,
    tall_cos_ref, tall_sin_ref, att_ref, gq_ref, gk_ref, gv_ref, halo_ref, dk_ref, dv_ref,
):
    step = pl.program_id(0)
    block = blocks - 1 - step
    continued = conts_ref[block]
    offset = pl.multiple_of(continued * SHORT, SHORT)
    tables = tuple(ref.at[pl.ds(offset, SHORT)] for ref in (cos_ref, minus_ref, plus_ref))
    now = lax.rem(step, 2)
    own = (dk_ref.at[now], dv_ref.at[now])
    before = (dk_ref.at[1 - now], dv_ref.at[1 - now])

    @pl.when(step == 0)
    def _():
        for ref in own:
            ref[...] = jnp.zeros_like(ref)

    for ref in before:
        ref[...] = jnp.zeros_like(ref)
    row = lax.broadcasted_iota(jnp.int32, (2 * count, count), 0)
    column = lax.broadcasted_iota(jnp.int32, (2 * count, count), 1)
    allowed = column <= jnp.where(row >= count, row - count, row)
    args = (q_ref, k_ref, v_ref, g_ref, kp_ref, vp_ref, tables, att_ref, gq_ref, *own, *before)

    def each(some, work):
        some = math.gcd(some, pairs)

        def body(i, carry):
            work([pl.ds(pl.multiple_of((i * some + j) * LANES, LANES), LANES) for j in range(some)])
            return carry

        lax.fori_loop(0, pairs // some, body, 0)

    pl.when(continued == 0)(lambda: each(2, lambda lanes: attend_rows(False, lanes, count, allowed, *args)))
    pl.when(continued != 0)(lambda: each(2, lambda lanes: attend_rows(True, lanes, count, allowed, *args)))
    turn = tuple(ref.at[:, pl.ds(offset, SHORT)] for ref in (tall_cos_ref, tall_sin_ref))

    def leave(lanes):
        for pair in lanes:
            gk_ref[:, pair] = unrotate_tall(own[0], pair, *[ref[...] for ref in turn])
            gv_ref[:, pair] = own[1][pair, :].astype(BF16).T

    each(1, leave)

    @pl.when(block == 0)
    def _():
        base = tuple(ref.at[:, pl.ds(0, SHORT)] for ref in (tall_cos_ref, tall_sin_ref))

        def leave_halo(lanes):
            for pair in lanes:
                halo_ref[0, :, pair] = unrotate_tall(before[0], pair, *[ref[...] for ref in base])
                halo_ref[1, :, pair] = before[1][pair, :].astype(BF16).T

        each(1, leave_halo)


def attend(conts, q, k, v, g, tables, tall, count):
    rows, head_width = q.shape
    blocks = rows // SHORT
    here = pl.BlockSpec((SHORT, head_width), lambda i, conts: (blocks - 1 - i, 0))
    after = pl.BlockSpec((SHORT, head_width), lambda i, conts: (blocks - i, 0))
    return pl.pallas_call(
        functools.partial(attend_kernel, blocks, head_width // LANES, count),
        grid_spec=pltpu.PrefetchScalarGridSpec(
            num_scalar_prefetch=1,
            grid=(blocks,),
            in_specs=[here, after, after, here, here, here] + [whole(table.shape) for table in (*tables, *tall)],
            out_specs=[here] * 4 + [held((2, SHORT, head_width))],
            scratch_shapes=[pltpu.VMEM((2, head_width, SHORT), F32)] * 2,
        ),
        out_shape=[shaped((rows, head_width), BF16)] * 4 + [shaped((2, SHORT, head_width), BF16)],
        compiler_params=params(),
        cost_estimate=BRIEF,
        name="attend",
    )(conts, q, k, v, g, k, v, *tables, *tall)


def settle_kernel(
    unit, tile, normed_ref, low_ref, grad_lows_ref, out_in_ref, att_ref, gq_ref, gk_ref, gv_ref, halo_ref, triple0_ref,
    triple1_ref, left_ref, output0_ref, output1_ref, right_ref, output_left_ref, out_ref, keep_ref, heads_ref,
    left_sums_ref, got_ref, send_ref, halo_got_ref, key_ref, value_ref, mixed_ref, triple_ref, output_ref, acc_ref,
    out_acc_ref, left_grad_ref, halo_sems, sems, load_sems,
):
    step = pl.program_id(0)
    per_device = got_ref.shape[1] // tile
    steps = unit * per_device
    halo_start = steps - SHORT // tile
    place, base = place_in_unit(unit)
    half = base // unit
    peers = unit_peers(unit)
    y_peer = chip_neighbours(unit)[1]
    halo_copies = []
    for j in range(SHORT // tile):
        part = pl.ds(j * tile, tile)
        halo_copies.append(
            pltpu.make_async_remote_copy(
                src_ref=halo_ref.at[:, part], dst_ref=halo_got_ref.at[:, part], send_sem=halo_sems.at[0, j],
                recv_sem=halo_sems.at[1, j], device_id=y_peer, device_id_type=MESH,
            )
        )
    copies = [
        [
            pltpu.make_async_remote_copy(
                src_ref=send_ref.at[s, pl.ds(t * tile, tile)], dst_ref=got_ref.at[s, pl.ds(t * tile, tile)],
                send_sem=sems.at[0, s, t], recv_sem=sems.at[1, s, t], device_id=peer, device_id_type=MESH,
            )
            for t in range(per_device)
        ]
        for s, peer in enumerate(peers)
    ]
    @pl.when(step == 0)
    def _():
        meet([y_peer, *peers])

        @pl.when(half == 1)
        def _():
            for copy in halo_copies:
                copy.start()

        for ref in (acc_ref, out_acc_ref, left_grad_ref):
            ref[...] = jnp.zeros_like(ref)

    load(
        step, load_sems,
        head_weights(
            unit, (triple0_ref, triple1_ref), right_ref, (output0_ref, output1_ref), output_left_ref, triple_ref,
            output_ref,
        ),
    )

    key_ref[...], value_ref[...] = gk_ref[...], gv_ref[...]
    for j, copy in enumerate(halo_copies):

        @pl.when((half == 0) & (step == halo_start + j))
        def _():
            copy.wait_recv()
            rows = pl.ds(j * tile, tile)
            count = output0_ref.shape[0]
            for ref, which in ((key_ref, 0), (value_ref, 1)):
                for here, there in ((pl.ds(0, count), pl.ds(count, count)), (pl.ds(count, count), pl.ds(0, count))):
                    ref[:, here] = (ref[:, here].astype(F32) + halo_got_ref[which, rows, there].astype(F32)).astype(BF16)

    normed = normed_ref[...]
    low = low_ref[...]
    grad_low_out = grad_lows_ref[:, :LANES]
    head_width = output0_ref.shape[0]
    first = low_lanes()
    for pair in range(2 * head_width // LANES):
        q, k, v = (ref[:, pair * LANES : (pair + 1) * LANES] for ref in (gq_ref, key_ref, value_ref))
        for part, value in enumerate((jnp.where(first, q, k), jnp.where(first, v, q), jnp.where(first, k, v))):
            mixed_ref[:, (3 * pair + part) * LANES : (3 * pair + part + 1) * LANES] = value
    mixed = mixed_ref[...]
    att = att_ref[...]
    width = normed.shape[1]
    backward = dot_nt(mixed, triple_ref[...])
    forward = dot_nn(att, output_ref[...])
    grad_low = backward[:, width:].astype(BF16)
    grad = (backward[:, :width] + dot_nt(grad_low, left_ref[...])).astype(BF16)
    out_ref[...] = out_in_ref[...] + forward[:, :width]
    low_att = forward[:, width:].astype(BF16)

    @pl.when(step // per_device == place)
    def _():
        keep_ref[:, :width] = grad
        keep_ref[:, width:] = low_att

    span = pl.ds(pl.multiple_of(lax.rem(step, per_device) * tile, tile), tile)
    for s in range(unit - 1):
        owner = lax.rem(place + unit - (s + 1), unit)

        @pl.when(step // per_device == owner)
        def _():
            send_ref[s, span, :width] = grad
            send_ref[s, span, width:] = low_att

        for t in range(per_device):
            pl.when(step == owner * per_device + t)(copies[s][t].start)

    acc_ref[...] += dot_tn(low, mixed)
    out_acc_ref[...] += dot_tn(grad_low_out, att)
    left_grad_ref[...] += dot_tn(grad_low, normed)

    @pl.when(step == steps - 1)
    def _():
        size = 3 * head_width
        for j in range(2):
            heads_ref[j, :, :size] = acc_ref[:, j * size : (j + 1) * size].astype(BF16)
            heads_ref[j, :, size:] = out_acc_ref[:, j * head_width : (j + 1) * head_width].astype(BF16)
        quarters(left_sums_ref, left_grad_ref[...])

        @pl.when(half == 1)
        def _():
            for copy in halo_copies:
                copy.wait_send()

        for group in copies:
            for copy in group:
                copy.wait()


def settle(unit, normed, low, grad_lows, out, heads, halo, triples, left, outputs, right, output_left, tile):
    rows, width = normed.shape
    own_rows = rows // unit
    head_width = outputs[0].shape[0]
    steps, per_device = rows // tile, own_rows // tile
    anywhere = pl.BlockSpec(memory_space=pl.ANY)

    def kept(i):
        return (jnp.clip(i - place_in_unit(unit)[0] * per_device, 0, per_device - 1), 0)

    return pl.pallas_call(
        functools.partial(settle_kernel, unit, tile),
        grid=(steps,),
        in_specs=[rows_of(tile, width), rows_of(tile, LANES), rows_of(tile, 2 * LANES), rows_of(tile, width)]
        + [rows_of(tile, 2 * head_width)] * 4
        + [anywhere]
        + [anywhere, anywhere, whole(left.shape), anywhere, anywhere, anywhere, anywhere],
        out_specs=[
            rows_of(tile, width),
            pl.BlockSpec((tile, width + LANES), kept),
            held((2, LANES, 4 * head_width)),
            held((2, 2, LANES, width // 4)),
            anywhere,
        ],
        scratch_shapes=[
            pltpu.VMEM((unit - 1, own_rows, width + LANES), BF16),
            pltpu.VMEM((2, SHORT, 2 * head_width), BF16),
            pltpu.VMEM((tile, 2 * head_width), BF16),
            pltpu.VMEM((tile, 2 * head_width), BF16),
            pltpu.VMEM((tile, 6 * head_width), BF16),
            pltpu.VMEM((width + LANES, 6 * head_width), BF16),
            pltpu.VMEM((2 * head_width, width + LANES), BF16),
            pltpu.VMEM((LANES, 6 * head_width), F32),
            pltpu.VMEM((LANES, 2 * head_width), F32),
            pltpu.VMEM((LANES, width), F32),
            pltpu.SemaphoreType.DMA((2, SHORT // tile)),
            pltpu.SemaphoreType.DMA((2, unit - 1, per_device)),
            pltpu.SemaphoreType.DMA((8,)),
        ],
        out_shape=[
            shaped((rows, width), F32),
            shaped((own_rows, width + LANES), BF16),
            shaped((2, LANES, 4 * head_width), BF16),
            shaped((2, 2, LANES, width // 4), BF16),
            shaped((unit - 1, own_rows, width + LANES), BF16),
        ],
        compiler_params=pltpu.CompilerParams(
            dimension_semantics=("arbitrary",), vmem_limit_bytes=VMEM_LIMIT, collective_id=5, has_side_effects=True
        ),
        cost_estimate=BRIEF,
        name="settle",
    )(normed, low, grad_lows, out, *heads, halo, *triples, left, *outputs, right, output_left)


FEED_ORDERS = ("xz", "zx", "xz", "zx")


def sum_kernel(size, feed_ref, both_ref, heads_ref, left_ref, feed_out_ref, both_out_ref, heads_out_ref, left_out_ref,
               cross_sems, local_sems, *refs):
    net = Net()
    meet([net.x_peer, net.y_peer, net.core_peer, *net.z_peers])
    locals_, crossing = [], []

    def hand_over(slot, full, out, first, second):
        for place, at in ((0, first), (1, second)):
            target = out.at[net.core, at]
            local = pltpu.make_async_copy(full.at[place], target, local_sems.at[slot, place])
            local.start()
            locals_.append(local)
            crossing.append(net.copy(full.at[place], target, cross_sems, 2 * slot + place, net.core_peer))
            net.start(crossing[-1:])

    split = len(sum_scratch("xz", size))
    feed_refs = [refs[j * split : (j + 1) * split] for j in range(len(FEED_ORDERS))]
    both_refs = refs[len(FEED_ORDERS) * split :]
    parts = split_columns(both_ref.shape[-1])
    per_part = (len(both_refs) - 3) // 2
    scratches = (both_refs[3 : 3 + per_part], both_refs[3 + per_part :])
    running = [sum_both(net, parts, both_ref, *both_refs[:3], scratches)]
    running += [
        sum_chunk(net, order, feed_ref.at[:, :, :, pl.ds(j * size, size)], feed_refs[j])
        for j, order in enumerate(FEED_ORDERS)
    ]

    def both_done():
        start = 0
        for j, (_, count) in enumerate(parts):
            columns = both_out_ref.at[:, :, :, :, :, pl.ds(start, count)]
            hand_over(j, scratches[j][5], columns, net.half, net.other_half)
            start += count

    def feed_done(j):
        columns = feed_out_ref.at[:, :, :, :, :, pl.ds(j * size, size)]
        hand_over(4 + j, feed_refs[j][5], columns, net.other_half, net.half)

    for k in range(max(len(stage) for stage in running)):
        for j, stage in enumerate(running):
            if k < len(stage):
                stage[k]()
            if k == len(stage) - 1:
                both_done() if j == 0 else feed_done(j - 1)
        if k == 0:
            hand_over(2, heads_ref, heads_out_ref, net.half, net.other_half)
            hand_over(3, left_ref, left_out_ref, net.half, net.other_half)
    for copy in locals_:
        copy.wait()
    for copy in crossing:
        copy.wait_recv()
    for copy in net.started:
        copy.wait_send()


def sum_all(feed, both, heads, left):
    arrays = (feed.reshape(SUM_ROWS + feed.shape[-1:]), both.reshape((2, 2) + SUM_ROWS + both.shape[-1:]), heads, left)
    size = feed.shape[-1] // len(FEED_ORDERS)
    slots = 4 + len(FEED_ORDERS)
    outs = [shaped((2, 2) + SUM_ROWS + array.shape[-1:], BF16) for array in arrays]
    results = pl.pallas_call(
        functools.partial(sum_kernel, size),
        out_shape=outs,
        in_specs=[pl.BlockSpec(memory_space=pltpu.VMEM)] * 4,
        out_specs=[pl.BlockSpec(memory_space=pl.ANY)] * 4,
        scratch_shapes=[pltpu.SemaphoreType.DMA((2, 2 * slots)), pltpu.SemaphoreType.DMA((slots, 2))]
        + [shape for order in FEED_ORDERS for shape in sum_scratch(order, size)]
        + both_scratch(split_columns(both.shape[-1])),
        compiler_params=pltpu.CompilerParams(
            collective_id=2, has_side_effects=True, vmem_limit_bytes=VMEM_LIMIT
        ),
        cost_estimate=BRIEF,
        name="sum_all",
    )(*arrays)
    return [value.reshape(2, 2, LANES, value.shape[-1]) for value in results]


def unpack_kernel(triple_width, feed_ref, both_ref, heads_ref, left_ref, triple_ref, output_ref, up_ref, down_ref,
                  triple_left_ref, up_left_ref, output_right_ref, down_right_ref, *norm_refs):
    triple_ref[...] = heads_ref[0, 0, :, :triple_width].astype(F32)
    output_ref[...] = heads_ref[0, 0, :, triple_width:].astype(F32).T
    hidden = up_ref.shape[1]
    up_ref[...] = feed_ref[0, 0, :, :hidden].astype(F32)
    down_ref[...] = feed_ref[0, 0, :, hidden:].astype(F32).T
    size = triple_left_ref.shape[0]
    triple_left_ref[...] = left_ref[0, 0].astype(F32).T
    up_left_ref[...] = both_ref[0, 0, :, :size].astype(F32).T
    output_right_ref[...] = both_ref[0, 0, :, size : 2 * size].astype(F32)
    down_right_ref[...] = both_ref[0, 0, :, 2 * size : 3 * size].astype(F32)
    for q, ref in enumerate(norm_refs):

        @pl.when(pl.program_id(0) == q)
        def _():
            ref[...] = both_ref[0, 0, : ref.shape[0], 3 * size :].astype(F32)


def unpack(feed, both, heads, left, triple_width):
    arrays = (feed, both, heads, left)
    hidden, quarter = feed.shape[-1] // 2, left.shape[-1]
    width, head_width = 4 * quarter, heads.shape[-1] - triple_width

    def tall(rows):
        return pl.BlockSpec((rows, LANES), lambda s: (s, 0))

    def wide(cols):
        return pl.BlockSpec((LANES, cols), lambda s: (0, s))

    return pl.pallas_call(
        functools.partial(unpack_kernel, triple_width),
        grid=(4,),
        in_specs=[
            pl.BlockSpec((1, 1) + value.shape[2:], lambda s: (lax.rem(s, 2), s // 2, 0, 0)) for value in arrays
        ],
        out_specs=[
            wide(triple_width), tall(head_width), wide(hidden), tall(hidden), tall(quarter), tall(quarter),
            wide(quarter), wide(quarter), *[held((width // LANES, LANES))] * 4,
        ],
        out_shape=[
            shaped((LANES, 4 * triple_width), F32),
            shaped((4 * head_width, LANES), F32),
            shaped((LANES, 4 * hidden), F32),
            shaped((4 * hidden, LANES), F32),
            shaped((width, LANES), F32),
            shaped((width, LANES), F32),
            shaped((LANES, width), F32),
            shaped((LANES, width), F32),
        ]
        + [shaped((width // LANES, LANES), F32)] * 4,
        compiler_params=params(),
        cost_estimate=BRIEF,
        name="unpack",
    )(*arrays)


def shards(
    ranks,
    groups,
    block_input,
    sequence_lengths,
    first_gain,
    first_shift,
    second_gain,
    second_shift,
    triple_weight,
    triple_left,
    triple_right,
    output_weight,
    output_left,
    output_right,
    expand_weight,
    expand_left,
    expand_right,
    shrink_weight,
    shrink_left,
    shrink_right,
    cotangent,
):
    unit = ranks // 2
    own_rows, width = block_input.shape
    rows = own_rows * unit
    blocks = rows // SHORT
    tile = math.gcd(own_rows, 256)
    triple_width = triple_weight.shape[1]
    head_width = output_weight.shape[0]
    hidden = expand_weight.shape[1]
    mp = lax.axis_index("mp")
    half = mp // unit
    place = lax.rem(mp, unit)
    far = lax.rem(mp + unit, ranks)
    swap = [(m, (m + unit) % ranks) for m in range(ranks)]

    tables = rotary_tables()
    beside = [[(d, d ^ bit) for d in range(groups)] for bit in (1, 2)]
    continues = find_flags(sequence_lengths[0])
    conts = lax.dynamic_slice_in_dim(continues, half * blocks, blocks, 0)
    gain1, shift1 = first_gain[None, :], first_shift[None, :]
    gain2, shift2 = second_gain[None, :], second_shift[None, :]

    (normed1, normed2, dy, low2, grad_lows, out, grad2, low_act, grad_low2, feed_sums, triple_far,
     output_far, x_halo, expand_half, shrink_half) = feed_first(
        unit, block_input, cotangent, (gain1, shift1, gain2, shift2), expand_weight, expand_left, expand_right,
        shrink_weight, shrink_left, output_right, shrink_right, triple_weight, output_weight, tile,
    )
    expand_piece = lax.ppermute(expand_half, "mp", swap)
    shrink_piece = lax.ppermute(shrink_half, "mp", swap)
    low1, q, k, v, g = project(
        unit, conts, x_halo, normed1, dy, grad_lows, gain1, shift1, (triple_weight, triple_far), triple_left,
        triple_right, (output_weight, output_far), output_left, tables, tile,
    )
    att, gq, gk, gv, halo = attend(conts, q, k, v, g, tables, tall_tables(), 256)
    expand_piece, shrink_piece, att = lax.optimization_barrier((expand_piece, shrink_piece, att))
    expand_other = lax.ppermute(expand_piece, "dp", beside[0])
    shrink_other = lax.ppermute(shrink_piece, "dp", beside[1])
    out, keep1, heads, left, got1 = settle(
        unit, normed1, low1, grad_lows, out, (att, gq, gk, gv), halo, (triple_weight, triple_far), triple_left,
        (output_weight, output_far), triple_right, output_left, tile,
    )
    hosted = ranks == 4 and groups == 8
    block_output, input_gradient, feed_sums, both, heads_sum, left_sum = feed_second(
        unit, normed2, low2, dy, grad_lows, out, grad2, low_act, grad_low2, block_input, keep1, got1, (gain1, gain2),
        output_right, shrink_right, (expand_piece, expand_other), expand_left, expand_right,
        (shrink_piece, shrink_other), shrink_left, feed_sums, heads, left, hosted, tile,
    )
    if hosted:
        (triple_right_sum, output_left_sum, expand_right_sum, shrink_left_sum, triple_left_sum, expand_left_sum,
         output_right_sum, shrink_right_sum, *norms) = unpack(
            *sum_all(feed_sums, both, heads_sum, left_sum), triple_width
        )
        norms = [value.reshape(width) for value in norms]
    else:

        def spread(*placed):
            size = placed[0][0].shape[1]
            wide = jnp.zeros((LANES, size * ranks), BF16)
            for value, shard in placed:
                wide = lax.dynamic_update_slice_in_dim(wide, value, shard * size, 1)
            return wide

        def joined(value):
            return value.transpose(2, 1, 0, 3).reshape(LANES, -1)

        def columns(value, start, size):
            return value.reshape(LANES, ranks, -1)[:, :, start : start + size].reshape(LANES, -1).astype(F32)

        heads, feed, left, both = lax.psum(
            (spread((heads[0], mp), (heads[1], far)), spread((feed_sums, far)), left, both), ("dp", "mp")
        )
        triple_right_sum = columns(heads, 0, triple_width)
        output_left_sum = columns(heads, triple_width, head_width).T
        expand_right_sum = columns(feed, 0, hidden)
        shrink_left_sum = columns(feed, hidden, hidden).T
        triple_left_sum = joined(left).astype(F32).T
        quarter = width // 4
        expand_left_sum = joined(both[..., :quarter]).astype(F32).T
        output_right_sum = joined(both[..., quarter : 2 * quarter]).astype(F32)
        shrink_right_sum = joined(both[..., 2 * quarter : 3 * quarter]).astype(F32)
        norms = both[:, :, : width // LANES, 3 * quarter :].transpose(1, 0, 2, 3).reshape(4, width).astype(F32)
    return (
        block_output,
        input_gradient,
        norms[0],
        norms[1],
        norms[2],
        norms[3],
        triple_left_sum,
        triple_right_sum,
        output_left_sum,
        output_right_sum,
        expand_left_sum,
        expand_right_sum,
        shrink_left_sum,
        shrink_right_sum,
    )


def solution(mesh):
    placed = (
        P(("dp", "mp"), None),
        P("dp", None),
        P(),
        P(),
        P(),
        P(),
        P(None, "mp"),
        P(),
        P(),
        P("mp", None),
        P(),
        P(),
        P(None, "mp"),
        P(),
        P(),
        P("mp", None),
        P(),
        P(),
        P(("dp", "mp"), None),
    )
    return jax.shard_map(
        functools.partial(shards, mesh.shape["mp"], mesh.shape["dp"]),
        mesh=mesh,
        in_specs=placed,
        out_specs=(P(("dp", "mp"), None), P(("dp", "mp"), None)) + (P(),) * 12,
        check_vma=False,
    )
```

profile of v0, /device:TPU:1, one launch (start us, length us, event | category | flops | bytes accessed | tf_op | source)
XLA Modules:
  0.0 238.4 jit_solution(17874888771207549369)
XLA Ops:
  0.7 41.0 %feed_first.1 = (bf16[1536,1024]{1,0:T(8,128)(2,1)}, bf16[1536,1024]{1,0:T(8,128)(2,1)}, bf16[1536,1024]{1,0:T(8,128)(2,1)}, bf16[1536,128]{1,0:T(8,128)(2,1)}, ...) custom-call(bf16[768,1024]{1,0:T(8,128)(2,1)} %x_ref.3, ...), custom_call_target="tpu_custom_call" | custom-call | flops 1 | bytes 1 | tf_op jit(solution)/shard_map/feed_first/pallas_call | solution.py:610
  41.7 3.5 %collective-permute-start = (bf16[512,1024]{1,0:T(8,128)(2,1)}, bf16[512,1024]{1,0:T(8,128)(2,1)S(1)}, u32[]{:S(2)}, u32[]{:S(2)}) collective-permute-start(bf16[512,1024]{1,0:T(8,128)(2,1)} %get-tuple-element.79), channel_id=1, source_target_pairs={{0,2},{1,3},{2,0},{3,1},{4,6},{5,7},{6,4},{7,5},{8,10},{9,11},{10,... | collective-permute-start | bytes 3145736 | tf_op jit(solution)/shard_map/ppermute | solution.py:1580
  45.2 0.1 collective-permute-start.1
  45.2 0.2 reduce-window_clone.1
  45.4 0.2 and_reduce_fusion
  45.6 0.1 dynamic_slice.3.conts_ref
  45.7 0.1 broadcast_in_dim.37
  45.8 0.1 reshape.78
  45.9 0.7 broadcast_in_dim.38.late_ref
  46.6 20.6 %project.1 = (bf16[1536,128]{1,0:T(8,128)(2,1)}, bf16[1536,512]{1,0:T(8,128)(2,1)}, bf16[2048,512]{1,0:T(8,128)(2,1)}, bf16[2048,512]{1,0:T(8,128)(2,1)}, bf16[1536,512]{1,0:T(8,128)(2,1)}) custom-call(bf16[512,1024]{1,0:T(8,128)(2,1)} %get-tuple-element.74.halo_ref, bf16[1536,1024]{1,0:T(8,128)(2,1)} %get-tuple-element.73.normed_ref, ...), custom_call_target="tpu_custom_call" | custom-call | flops 1 | bytes 1 | tf_op jit(solution)/shard_map/project/pallas_call | solution.py:1024
  67.2 31.2 %attend.1 = (bf16[1536,512]{1,0:T(8,128)(2,1)}, bf16[1536,512]{1,0:T(8,128)(2,1)}, bf16[1536,512]{1,0:T(8,128)(2,1)}, bf16[1536,512]{1,0:T(8,128)(2,1)}, bf16[2,512,512]{2,1,0:T(8,128)(2,1)}) custom-call(s32[3]{0:T(128)} %copy-done.6, bf16[1536,512]{1,0:T(8,128)(2,1)} %get-tuple-element.81.q_ref, bf16[2048,512]{1,0:T(8,128)(2,1)} %get-tuple-element.82.k_ref.kp_ref, ...), custom_call_target="tpu_custom_call" | custom-call | flops 1 | bytes 1 | tf_op jit(solution)/shard_map/attend/pallas_call | solution.py:1201
  98.4 0.0 copy-start.3
  98.4 1.3 collective-permute-start.2
  99.7 0.2 collective-permute-start.3
  99.9 42.3 %settle.1 = (f32[1536,1024]{1,0:T(8,128)}, bf16[768,1152]{1,0:T(8,128)(2,1)}, bf16[2,128,1024]{2,1,0:T(8,128)(2,1)}, bf16[2,2,128,256]{3,2,1,0:T(8,128)(2,1)}, bf16[1,768,1152]{2,1,0:T(8,128)(2,1)}) custom-call(bf16[1536,1024]{1,0:T(8,128)(2,1)} %get-tuple-element.73.normed_ref, bf16[1536,128]{1,0:T(8,128)(2,1)} %get-tuple-element.77.low_ref, ...), custom_call_target="tpu_custom_call" | custom-call | flops 1 | bytes 1 | tf_op jit(solution)/shard_map/settle/pallas_call | solution.py:1350
  142.3 0.0 copy-start.5
  142.3 0.9 copy-done.4
  143.2 0.3 copy-done.5
  143.6 40.9 %feed_second.1 = (bf16[768,1024]{1,0:T(8,128)(2,1)}, f32[768,1024]{1,0:T(8,128)}, bf16[128,2048]{1,0:T(8,128)(2,1)}, bf16[2,2,128,896]{3,2,1,0:T(8,128)(2,1)}, b...) custom-call(bf16[1536,1024]{1,0:T(8,128)(2,1)} %get-tuple-element.69.normed_ref, ...), custom_call_target="tpu_custom_call" | custom-call | flops 1 | bytes 1 | tf_op jit(solution)/shard_map/feed_second/pallas_call | solution.py:878
  184.4 43.5 %sum_all.1 = (bf16[2,2,2,4,16,2048]{5,4,3,2,1,0:T(8,128)(2,1)}, bf16[2,2,2,4,16,896]{5,4,3,2,1,0:T(8,128)(2,1)}, bf16[2,2,2,4,16,1024]{5,4,3,2,1,0:T(8,128)(2,1)}, bf16[2,2,2,4,16,256]{5,4,3,2,1,0:T(8,128)(2,1)}) custom-call(bf16[2,4,16,2048]{3,2,1,0:T(8,128)(2,1)} %bitcast.25, bf16[2,2,2,4,16,896]{5,4,3,2,1,0:T(8,128)(2,1)} %bitcast.23, ...), custom_call_target="tpu_custom_call" | custom-call | flops 1 | bytes 1 | tf_op jit(solution)/shard_map/sum_all/pallas_call | solution.py:1457
  228.0 6.4 %unpack.1 = (f32[128,3072]{1,0:T(8,128)}, f32[1024,128]{1,0:T(8,128)}, f32[128,4096]{1,0:T(8,128)}, f32[4096,128]{1,0:T(8,128)}, f32[1024,128]{1,0:T(8,128)}, /*...) custom-call(bf16[2,2,128,2048]{3,2,1,0:T(8,128)(2,1)} %bitcast.20, ...), custom_call_target="tpu_custom_call" | custom-call | flops 1 | bytes 1 | tf_op jit(solution)/shard_map/unpack/pallas_call | solution.py:1504
  234.3 1.1 copy.40
  235.5 1.3 copy-done
  236.8 1.7 copy.41
  (20 shorter events, 0.1 us)
Async XLA Ops:
  0.6 44.6 %copy-start.7 = (s32[1,6]{1,0:T(1,128)S(1)}, s32[1,6]{1,0:T(1,128)}, u32[]{:S(2)}) copy-start(s32[1,6]{1,0:T(1,128)} %param.25) | copy-start | bytes 76
  41.7 56.7 %collective-permute-start = (bf16[512,1024]{1,0:T(8,128)(2,1)}, bf16[512,1024]{1,0:T(8,128)(2,1)S(1)}, u32[]{:S(2)}, u32[]{:S(2)}) collective-permute-start(bf16[512,1024]{1,0:T(8,128)(2,1)} %get-tuple-element.79), channel_id=1, source_target_pairs={{0,2},{1,3},{2,0},{3,1},{4,6},{5,7},{6,4},{7,5},{8,10},{9,11},{10,... | collective-permute-start | bytes 3145736 | tf_op jit(solution)/shard_map/ppermute | solution.py:1580
  45.2 53.3 %collective-permute-start.1 = (bf16[512,1024]{1,0:T(8,128)(2,1)}, bf16[512,1024]{1,0:T(8,128)(2,1)S(1)}, u32[]{:S(2)}, u32[]{:S(2)}) collective-permute-start(bf16[512,1024]{1,0:T(8,128)(2,1)} %get-tuple-element.80), channel_id=1, source_target_pairs={{0,2},{1,3},{2,0},{3,1},{4,6},{5,7},{6,4},{7,5},{8,10},{9,11},{10,... | collective-permute-start | bytes 3145736 | tf_op jit(solution)/shard_map/ppermute | solution.py:1581
  45.7 21.4 %copy-start.6 = (s32[3]{0:T(128)}, s32[3]{0:T(128)S(1)}, u32[]{:S(2)}) copy-start(s32[3]{0:T(128)S(1)} %dynamic_slice.3.conts_ref) | copy-start | bytes 40
  98.4 43.8 %copy-start.2 = (bf16[512,1024]{1,0:T(8,128)(2,1)}, bf16[512,1024]{1,0:T(8,128)(2,1)S(1)}, u32[]{:S(2)}) copy-start(bf16[512,1024]{1,0:T(8,128)(2,1)S(1)} %collective-permute-done.up0_ref) | copy-start | bytes 3145732
  98.4 43.8 %copy-start.3 = (bf16[512,1024]{1,0:T(8,128)(2,1)}, bf16[512,1024]{1,0:T(8,128)(2,1)S(1)}, u32[]{:S(2)}) copy-start(bf16[512,1024]{1,0:T(8,128)(2,1)S(1)} %collective-permute-done.1.down0_ref) | copy-start | bytes 3145732
  98.4 43.8 %collective-permute-start.2 = (bf16[512,1024]{1,0:T(8,128)(2,1)S(1)}, bf16[512,1024]{1,0:T(8,128)(2,1)S(1)}, u32[]{:S(2)}, u32[]{:S(2)}) collective-permute-start(bf16[512,1024]{1,0:T(8,128)(2,1)S(1)} %collective-permute-done.up0_ref), channel_id=1, source_target_pairs={{0,4},{4,0},{8,12},{12,8},{16,20},{20,16},{24,28},{28,24},{1,5},{5... | collective-permute-start | bytes 3145736 | tf_op jit(solution)/shard_map/ppermute | solution.py:1588
  99.7 42.5 %collective-permute-start.3 = (bf16[512,1024]{1,0:T(8,128)(2,1)S(1)}, bf16[512,1024]{1,0:T(8,128)(2,1)S(1)}, u32[]{:S(2)}, u32[]{:S(2)}) collective-permute-start(bf16[512,1024]{1,0:T(8,128)(2,1)S(1)} %collective-permute-done.1.down0_ref), channel_id=1, source_target_pairs={{0,8},{4,12},{8,0},{12,4},{16,24},{20,28},{24,16},{28,20},{1,9},{5... | collective-permute-start | bytes 3145736 | tf_op jit(solution)/shard_map/ppermute | solution.py:1589
  142.2 1.0 copy-start.4
  142.3 1.3 copy-start.5
  227.9 6.4 %copy-start.1 = (bf16[768,1024]{1,0:T(8,128)(2,1)S(1)}, bf16[768,1024]{1,0:T(8,128)(2,1)}, u32[]{:S(2)}) copy-start(bf16[768,1024]{1,0:T(8,128)(2,1)} %get-tuple-element.138) | copy-start | bytes 4718596
  234.3 2.5 %copy-start = (f32[768,1024]{1,0:T(8,128)S(1)}, f32[768,1024]{1,0:T(8,128)}, u32[]{:S(2)}) copy-start(f32[768,1024]{1,0:T(8,128)} %get-tuple-element.139) | copy-start | bytes 9437188
where the time goes:
time: 239 us; the launch traced here: 238 us
  Pallas kernels  226 us (95%)
  local copies, waits for them, and re-layouts  6.35 us (3%)
  starting transfers between devices  4.99 us (2%)
    pallas_call x1, Pallas kernels, sum_all(): pl.pallas_call(functools.partial(sum_kernel, size), out_shape=outs, in_sp...  43.5 us
    pallas_call x1, Pallas kernels, settle(): pl.pallas_call(functools.partial(settle_kernel, unit, tile), grid=(steps,...  42.3 us
    pallas_call x1, Pallas kernels, feed_first(): pl.pallas_call(functools.partial(feed_first_kernel, unit, tile), grid=(st...  41 us
    pallas_call x1, Pallas kernels, feed_second(): pl.pallas_call(functools.partial(feed_second_kernel, unit, tile), grid=(s...  40.9 us
    pallas_call x1, Pallas kernels, attend(): pl.pallas_call(functools.partial(attend_kernel, blocks, head_width // LAN...  31.2 us
    pallas_call x1, Pallas kernels, project(): pl.pallas_call(functools.partial(project_kernel, unit, main_tiles), grid=...  20.6 us
    pallas_call x1, Pallas kernels, unpack(): pl.pallas_call(functools.partial(unpack_kernel, triple_width), grid=(4,),...  6.36 us
    unnamed x18, local copies, waits for them, and re-layouts  5.42 us
  transfers between devices with their start and end apart: 4, of which 0 were waited for; matrix products, arithmetic and copies ran while one was open for 1% of the time, Pallas kernels for 39%

commit v1 on v0

--- a/solution.py
+++ b/solution.py
@@ -370,25 +370,40 @@
     return lax.rem(dp, 2), lax.rem(dp // 2, 2)
 
 
-def courier(unit, pairs, chunks, y_sems, x_sems):
-    lead, y_peer, x_peer = chip_neighbours(unit)
-    over_y, over_x = [], []
+def group_neighbours():
+    dp, mp = lax.axis_index("dp"), lax.axis_index("mp")
+    first, second = leads()
+    return (dp + 1 - 2 * first, mp), (dp + 2 - 4 * second, mp)
+
+
+def courier(unit, pairs, chunks, sems):
+    first, second = leads()
+    mine = first + 2 * second
+    y_peer = chip_neighbours(unit)[1]
+    x_peer, z_peer = group_neighbours()
+    over_y, once, twice = [], [], []
     for k in range(chunks):
+        over_y.append([])
+        once.append([])
+        twice.append([])
         for j, (own, far) in enumerate(pairs):
-            count = own.shape[0] // 2 // chunks
-            span = pl.ds(pl.multiple_of((lead * chunks + k) * count, count), count)
-            for src, sems, peer, group in ((own, y_sems, y_peer, over_y), (far, x_sems, x_peer, over_x)):
-                group.append(
-                    pltpu.make_async_remote_copy(
-                        src_ref=src.at[span],
-                        dst_ref=far.at[span],
-                        send_sem=sems.at[0, k, j],
-                        recv_sem=sems.at[1, k, j],
-                        device_id=peer,
-                        device_id_type=MESH,
-                    )
+            count = own.shape[0] // 4 // chunks
+
+            def copy(kind, src, dst, quarter, start, size, peer, k=k, j=j, count=count):
+                span = pl.ds(pl.multiple_of((quarter * chunks + k) * count + start, size), size)
+                return pltpu.make_async_remote_copy(
+                    src_ref=src.at[span], dst_ref=dst.at[span], send_sem=sems.at[0, kind, k, j],
+                    recv_sem=sems.at[1, kind, k, j], device_id=peer, device_id_type=MESH,
                 )
-    return over_y, over_x
+
+            by_x, by_z = mine + 1 - 2 * first, mine + 2 - 4 * second
+            over_y[-1].append(copy(0, own, far, mine, 0, count, y_peer))
+            once[-1] += [copy(1, far, far, mine, 0, count, x_peer), copy(2, far, far, mine, 0, count, z_peer)]
+            twice[-1] += [
+                copy(3, far, far, by_x, 0, count // 2, z_peer),
+                copy(4, far, far, by_z, count // 2, count // 2, x_peer),
+            ]
+    return over_y, once, twice
 
 
 def meet(peers):
@@ -437,7 +452,7 @@
     down_own_ref, down_left_ref, output_right_ref, down_right_ref, x_all_ref, dy_all_ref, triple_ref, output_ref, normed1_ref,
     normed_ref, dy_full_ref, low_ref, grad_lows_ref, out_ref, grad_ref, low_act_ref, grad_low_ref, sums_ref,
     triple_far_ref, output_far_ref, halo_ref, up_half_ref, down_half_ref, act_ref, gh_ref, up_ref, down_ref, acc_ref,
-    xs_ref, x_got_ref, dy_got_ref, y_sems, x_sems, unit_sems, halo_y_sems, halo_unit_sems, local_sems, load_sems,
+    xs_ref, x_got_ref, dy_got_ref, courier_sems, unit_sems, halo_y_sems, halo_unit_sems, local_sems, load_sems,
 ):
     step = pl.program_id(0)
     width, hidden = up_own_ref.shape
@@ -450,12 +465,12 @@
     own_rows = x_all_ref.shape[0]
     per_device = own_rows // tile
     steps = unit * per_device
-    chunks = y_sems.shape[1]
+    chunks = courier_sems.shape[2]
     place, base = place_in_unit(unit)
     half = base // unit
     peers = unit_peers(unit)
-    over_y, over_x = courier(
-        unit, ((triple_ref, triple_far_ref), (output_ref, output_far_ref)), chunks, y_sems, x_sems
+    over_y, once, twice = courier(
+        unit, ((triple_ref, triple_far_ref), (output_ref, output_far_ref)), chunks, courier_sems
     )
     halo = halo_copies(unit, x_all_ref, halo_ref, halo_y_sems, halo_unit_sems)
     rows_out = [
@@ -479,9 +494,12 @@
 
     @pl.when(step == 0)
     def _():
-        meet([*chip_neighbours(unit)[1:], *peers])
-        for copy in rows_out + over_y:
+        meet([chip_neighbours(unit)[1], *group_neighbours(), *peers])
+        for copy in rows_out:
             copy.start()
+        for copies in over_y:
+            for copy in copies:
+                copy.start()
 
     for holder, copy, _ in halo:
         pl.when((step == 0) & (half == 0) & (place == holder))(copy.start)
@@ -514,11 +532,21 @@
 
     for k in range(chunks):
 
-        @pl.when(step == min(k + 1, steps - 1))
+        @pl.when(step == min(k + 2, steps - 1))
         def _():
-            for j in (2 * k, 2 * k + 1):
-                over_y[j].wait_recv()
-                over_x[j].start()
+            for copy in over_y[k]:
+                copy.wait_recv()
+            for copy in once[k]:
+                copy.start()
+
+    for k in range(chunks):
+
+        @pl.when(step == min(k + 4, steps - 1))
+        def _():
+            for copy in once[k]:
+                copy.wait_recv()
+            for copy in twice[k]:
+                copy.start()
 
     x = xs_ref[...].astype(F32)
     center = x - jnp.mean(x, axis=-1, keepdims=True)
@@ -584,9 +612,14 @@
 
             for s in range(1, unit):
                 pl.when((half == 1) & (place == (holder + s) % unit))(spread_copies[s - 1].wait_recv)
-        for copy in rows_out + over_y:
+        for copy in rows_out:
             copy.wait_send()
-        for copy in over_x + kept_halves:
+        for k in range(chunks):
+            for copy in over_y[k] + once[k]:
+                copy.wait_send()
+            for copy in twice[k]:
+                copy.wait()
+        for copy in kept_halves:
             copy.wait()
 
 
@@ -596,7 +629,7 @@
     rows = own_rows * unit
     hidden = up.shape[1]
     steps, per_device = rows // tile, own_rows // tile
-    chunks = math.gcd(4, output.shape[0] // 32)
+    chunks = math.gcd(2, output.shape[0] // 128)
     halo_chunks = SHORT // math.gcd(own_rows, 128)
     anywhere = pl.BlockSpec(memory_space=pl.ANY)
     here = pl.BlockSpec((tile, width), lambda i: (jnp.minimum(i, per_device - 1), 0))
@@ -644,8 +677,7 @@
             pltpu.VMEM((tile, width), BF16),
             pltpu.VMEM((unit - 1, own_rows, width), BF16),
             pltpu.VMEM((unit - 1, own_rows, width), BF16),
-            pltpu.SemaphoreType.DMA((2, chunks, 2)),
-            pltpu.SemaphoreType.DMA((2, chunks, 2)),
+            pltpu.SemaphoreType.DMA((2, 5, chunks, 2)),
             pltpu.SemaphoreType.DMA((2, 2, unit - 1)),
             pltpu.SemaphoreType.DMA((2, halo_chunks)),
             pltpu.SemaphoreType.DMA((2, halo_chunks, unit - 1)),

time: 239 us -> 236 us (0.987)
  Pallas kernels: 226 us -> 216 us
  starting transfers between devices: 4.99 us -> 12 us
    ppermute x1, starting transfers between devices: 1.27 us -> 7.68 us  [shards(): expand_other = lax.ppermute(expand_piece, 'dp', beside[0])]
    pallas_call x1, Pallas kernels: 31.2 us -> 24.8 us  [attend(): pl.pallas_call(functools.partial(attend_kernel, blocks, head_width // LAN...]
    pallas_call x1, Pallas kernels: 41 us -> 37.1 us  [feed_first(): pl.pallas_call(functools.partial(feed_first_kernel, unit, tile), grid=(st...]
    pallas_call x1, Pallas kernels: 42.3 us -> 39.4 us  [settle(): pl.pallas_call(functools.partial(settle_kernel, unit, tile), grid=(steps,...]
    pallas_call x1, Pallas kernels: 40.9 us -> 43.3 us  [feed_second(): pl.pallas_call(functools.partial(feed_second_kernel, unit, tile), grid=(s...]
  transfers between devices with their start and end apart: 4 -> 4, of which waited for: 0 -> 0; matrix products, arithmetic and copies ran while one was open for 1% -> 1% of each run, Pallas kernels for 39% -> 36%
where the time goes in v1:
time: 236 us
  Pallas kernels  216 us (92%)
  starting transfers between devices  12 us (5%)
  local copies, waits for them, and re-layouts  6.35 us (3%)
    pallas_call x1, Pallas kernels, sum_all(): pl.pallas_call(functools.partial(sum_kernel, size), out_shape=outs, in_sp...  44.3 us
    pallas_call x1, Pallas kernels, feed_second(): pl.pallas_call(functools.partial(feed_second_kernel, unit, tile), grid=(s...  43.3 us
    pallas_call x1, Pallas kernels, settle(): pl.pallas_call(functools.partial(settle_kernel, unit, tile), grid=(steps,...  39.4 us
    pallas_call x1, Pallas kernels, feed_first(): pl.pallas_call(functools.partial(feed_first_kernel, unit, tile), grid=(st...  37.1 us
    pallas_call x1, Pallas kernels, attend(): pl.pallas_call(functools.partial(attend_kernel, blocks, head_width // LAN...  24.8 us
    pallas_call x1, Pallas kernels, project(): pl.pallas_call(functools.partial(project_kernel, unit, main_tiles), grid=...  20.6 us
    ppermute x1, starting transfers between devices, shards(): expand_other = lax.ppermute(expand_piece, 'dp', beside[0])  7.68 us
    pallas_call x1, Pallas kernels, unpack(): pl.pallas_call(functools.partial(unpack_kernel, triple_width), grid=(4,),...  6.36 us
  transfers between devices with their start and end apart: 4, of which 0 were waited for; matrix products, arithmetic and copies ran while one was open for 1% of the time, Pallas kernels for 36%

profile of v1, /device:TPU:1, one launch (start us, length us, event | category | flops | bytes accessed | tf_op | source)
XLA Modules:
  0.0 235.5 jit_solution(17510625528728874103)
XLA Ops:
  0.7 37.1 %feed_first.1 = (bf16[1536,1024]{1,0:T(8,128)(2,1)}, bf16[1536,1024]{1,0:T(8,128)(2,1)}, bf16[1536,1024]{1,0:T(8,128)(2,1)}, bf16[1536,128]{1,0:T(8,128)(2,1)}, ...) custom-call(bf16[768,1024]{1,0:T(8,128)(2,1)} %x_ref.3, ...), custom_call_target="tpu_custom_call" | custom-call | flops 1 | bytes 1 | tf_op jit(solution)/shard_map/feed_first/pallas_call | solution.py:643
  37.8 3.6 %collective-permute-start = (bf16[512,1024]{1,0:T(8,128)(2,1)}, bf16[512,1024]{1,0:T(8,128)(2,1)S(1)}, u32[]{:S(2)}, u32[]{:S(2)}) collective-permute-start(bf16[512,1024]{1,0:T(8,128)(2,1)} %get-tuple-element.79), channel_id=1, source_target_pairs={{0,2},{1,3},{2,0},{3,1},{4,6},{5,7},{6,4},{7,5},{8,10},{9,11},{10,... | collective-permute-start | bytes 3145736 | tf_op jit(solution)/shard_map/ppermute | solution.py:1612
  41.4 0.1 collective-permute-start.1
  41.5 0.2 reduce-window_clone.1
  41.6 0.2 and_reduce_fusion
  41.8 0.1 dynamic_slice.3.conts_ref
  41.9 0.1 broadcast_in_dim.37
  42.0 0.1 reshape.78
  42.1 0.7 broadcast_in_dim.38.late_ref
  42.8 20.6 %project.1 = (bf16[1536,128]{1,0:T(8,128)(2,1)}, bf16[1536,512]{1,0:T(8,128)(2,1)}, bf16[2048,512]{1,0:T(8,128)(2,1)}, bf16[2048,512]{1,0:T(8,128)(2,1)}, bf16[1536,512]{1,0:T(8,128)(2,1)}) custom-call(bf16[512,1024]{1,0:T(8,128)(2,1)} %get-tuple-element.74.halo_ref, bf16[1536,1024]{1,0:T(8,128)(2,1)} %get-tuple-element.73.normed_ref, ...), custom_call_target="tpu_custom_call" | custom-call | flops 1 | bytes 1 | tf_op jit(solution)/shard_map/project/pallas_call | solution.py:1056
  63.4 24.8 %attend.1 = (bf16[1536,512]{1,0:T(8,128)(2,1)}, bf16[1536,512]{1,0:T(8,128)(2,1)}, bf16[1536,512]{1,0:T(8,128)(2,1)}, bf16[1536,512]{1,0:T(8,128)(2,1)}, bf16[2,512,512]{2,1,0:T(8,128)(2,1)}) custom-call(s32[3]{0:T(128)} %copy-done.6, bf16[1536,512]{1,0:T(8,128)(2,1)} %get-tuple-element.81.q_ref, bf16[2048,512]{1,0:T(8,128)(2,1)} %get-tuple-element.82.k_ref.kp_ref, ...), custom_call_target="tpu_custom_call" | custom-call | flops 1 | bytes 1 | tf_op jit(solution)/shard_map/attend/pallas_call | solution.py:1233
  88.2 0.0 copy-start.2
  88.2 0.0 copy-start.3
  88.2 7.7 %collective-permute-start.2 = (bf16[512,1024]{1,0:T(8,128)(2,1)S(1)}, bf16[512,1024]{1,0:T(8,128)(2,1)S(1)}, u32[]{:S(2)}, u32[]{:S(2)}) collective-permute-start(bf16[512,1024]{1,0:T(8,128)(2,1)S(1)} %collective-permute-done.up0_ref), channel_id=1, source_target_pairs={{0,4},{4,0},{8,12},{12,8},{16,20},{20,16},{24,28},{28,24},{1,5},{5... | collective-permute-start | bytes 3145736 | tf_op jit(solution)/shard_map/ppermute | solution.py:1620
  95.9 0.7 collective-permute-start.3
  96.6 39.4 %settle.1 = (f32[1536,1024]{1,0:T(8,128)}, bf16[768,1152]{1,0:T(8,128)(2,1)}, bf16[2,128,1024]{2,1,0:T(8,128)(2,1)}, bf16[2,2,128,256]{3,2,1,0:T(8,128)(2,1)}, bf16[1,768,1152]{2,1,0:T(8,128)(2,1)}) custom-call(bf16[1536,1024]{1,0:T(8,128)(2,1)} %get-tuple-element.73.normed_ref, bf16[1536,128]{1,0:T(8,128)(2,1)} %get-tuple-element.77.low_ref, ...), custom_call_target="tpu_custom_call" | custom-call | flops 1 | bytes 1 | tf_op jit(solution)/shard_map/settle/pallas_call | solution.py:1382
  136.1 0.9 copy-done.4
  137.0 0.3 copy-done.5
  137.3 43.3 %feed_second.1 = (bf16[768,1024]{1,0:T(8,128)(2,1)}, f32[768,1024]{1,0:T(8,128)}, bf16[128,2048]{1,0:T(8,128)(2,1)}, bf16[2,2,128,896]{3,2,1,0:T(8,128)(2,1)}, b...) custom-call(bf16[1536,1024]{1,0:T(8,128)(2,1)} %get-tuple-element.69.normed_ref, ...), custom_call_target="tpu_custom_call" | custom-call | flops 1 | bytes 1 | tf_op jit(solution)/shard_map/feed_second/pallas_call | solution.py:910
  180.7 44.3 %sum_all.1 = (bf16[2,2,2,4,16,2048]{5,4,3,2,1,0:T(8,128)(2,1)}, bf16[2,2,2,4,16,896]{5,4,3,2,1,0:T(8,128)(2,1)}, bf16[2,2,2,4,16,1024]{5,4,3,2,1,0:T(8,128)(2,1)}, bf16[2,2,2,4,16,256]{5,4,3,2,1,0:T(8,128)(2,1)}) custom-call(bf16[2,4,16,2048]{3,2,1,0:T(8,128)(2,1)} %bitcast.25, bf16[2,2,2,4,16,896]{5,4,3,2,1,0:T(8,128)(2,1)} %bitcast.23, ...), custom_call_target="tpu_custom_call" | custom-call | flops 1 | bytes 1 | tf_op jit(solution)/shard_map/sum_all/pallas_call | solution.py:1489
  225.0 6.4 %unpack.1 = (f32[128,3072]{1,0:T(8,128)}, f32[1024,128]{1,0:T(8,128)}, f32[128,4096]{1,0:T(8,128)}, f32[4096,128]{1,0:T(8,128)}, f32[1024,128]{1,0:T(8,128)}, /*...) custom-call(bf16[2,2,128,2048]{3,2,1,0:T(8,128)(2,1)} %bitcast.20, ...), custom_call_target="tpu_custom_call" | custom-call | flops 1 | bytes 1 | tf_op jit(solution)/shard_map/unpack/pallas_call | solution.py:1536
  231.4 1.1 copy.40
  232.5 1.3 copy-done
  233.8 1.7 copy.41
  (20 shorter events, 0.1 us)
Async XLA Ops:
  0.6 40.8 %copy-start.7 = (s32[1,6]{1,0:T(1,128)S(1)}, s32[1,6]{1,0:T(1,128)}, u32[]{:S(2)}) copy-start(s32[1,6]{1,0:T(1,128)} %param.25) | copy-start | bytes 76
  37.8 50.4 %collective-permute-start = (bf16[512,1024]{1,0:T(8,128)(2,1)}, bf16[512,1024]{1,0:T(8,128)(2,1)S(1)}, u32[]{:S(2)}, u32[]{:S(2)}) collective-permute-start(bf16[512,1024]{1,0:T(8,128)(2,1)} %get-tuple-element.79), channel_id=1, source_target_pairs={{0,2},{1,3},{2,0},{3,1},{4,6},{5,7},{6,4},{7,5},{8,10},{9,11},{10,... | collective-permute-start | bytes 3145736 | tf_op jit(solution)/shard_map/ppermute | solution.py:1612
  41.4 46.9 %collective-permute-start.1 = (bf16[512,1024]{1,0:T(8,128)(2,1)}, bf16[512,1024]{1,0:T(8,128)(2,1)S(1)}, u32[]{:S(2)}, u32[]{:S(2)}) collective-permute-start(bf16[512,1024]{1,0:T(8,128)(2,1)} %get-tuple-element.80), channel_id=1, source_target_pairs={{0,2},{1,3},{2,0},{3,1},{4,6},{5,7},{6,4},{7,5},{8,10},{9,11},{10,... | collective-permute-start | bytes 3145736 | tf_op jit(solution)/shard_map/ppermute | solution.py:1613
  41.9 21.4 %copy-start.6 = (s32[3]{0:T(128)}, s32[3]{0:T(128)S(1)}, u32[]{:S(2)}) copy-start(s32[3]{0:T(128)S(1)} %dynamic_slice.3.conts_ref) | copy-start | bytes 40
  88.2 47.8 %copy-start.2 = (bf16[512,1024]{1,0:T(8,128)(2,1)}, bf16[512,1024]{1,0:T(8,128)(2,1)S(1)}, u32[]{:S(2)}) copy-start(bf16[512,1024]{1,0:T(8,128)(2,1)S(1)} %collective-permute-done.up0_ref) | copy-start | bytes 3145732
  88.2 47.8 %copy-start.3 = (bf16[512,1024]{1,0:T(8,128)(2,1)}, bf16[512,1024]{1,0:T(8,128)(2,1)S(1)}, u32[]{:S(2)}) copy-start(bf16[512,1024]{1,0:T(8,128)(2,1)S(1)} %collective-permute-done.1.down0_ref) | copy-start | bytes 3145732
  88.2 47.8 %collective-permute-start.2 = (bf16[512,1024]{1,0:T(8,128)(2,1)S(1)}, bf16[512,1024]{1,0:T(8,128)(2,1)S(1)}, u32[]{:S(2)}, u32[]{:S(2)}) collective-permute-start(bf16[512,1024]{1,0:T(8,128)(2,1)S(1)} %collective-permute-done.up0_ref), channel_id=1, source_target_pairs={{0,4},{4,0},{8,12},{12,8},{16,20},{20,16},{24,28},{28,24},{1,5},{5... | collective-permute-start | bytes 3145736 | tf_op jit(solution)/shard_map/ppermute | solution.py:1620
  95.9 40.1 %collective-permute-start.3 = (bf16[512,1024]{1,0:T(8,128)(2,1)S(1)}, bf16[512,1024]{1,0:T(8,128)(2,1)S(1)}, u32[]{:S(2)}, u32[]{:S(2)}) collective-permute-start(bf16[512,1024]{1,0:T(8,128)(2,1)S(1)} %collective-permute-done.1.down0_ref), channel_id=1, source_target_pairs={{0,8},{4,12},{8,0},{12,4},{16,24},{20,28},{24,16},{28,20},{1,9},{5... | collective-permute-start | bytes 3145736 | tf_op jit(solution)/shard_map/ppermute | solution.py:1621
  136.0 1.0 copy-start.4
  136.0 1.3 copy-start.5
  225.0 6.4 %copy-start.1 = (bf16[768,1024]{1,0:T(8,128)(2,1)S(1)}, bf16[768,1024]{1,0:T(8,128)(2,1)}, u32[]{:S(2)}) copy-start(bf16[768,1024]{1,0:T(8,128)(2,1)} %get-tuple-element.138) | copy-start | bytes 4718596
  231.4 2.5 %copy-start = (f32[768,1024]{1,0:T(8,128)S(1)}, f32[768,1024]{1,0:T(8,128)}, u32[]{:S(2)}) copy-start(f32[768,1024]{1,0:T(8,128)} %get-tuple-element.139) | copy-start | bytes 9437188

commit v2 on v1

--- a/solution.py
+++ b/solution.py
@@ -330,13 +330,15 @@
     return ref.at[pl.ds(pl.multiple_of(shard * size, size), size)]
 
 
-def load(step, sems, pairs):
+def load(step, sems, pairs, between=None):
     copies = [pltpu.make_async_copy(src, dst, sems.at[j]) for j, (src, dst) in enumerate(pairs)]
 
     @pl.when(step == 0)
     def _():
         for copy in copies:
             copy.start()
+        if between is not None:
+            between()
         for copy in copies:
             copy.wait()
 
@@ -492,18 +494,19 @@
         for j, (lead, src, dst) in enumerate(zip(leads(), (up_ref, down_ref), (up_half_ref, down_half_ref)))
     ]
 
-    @pl.when(step == 0)
-    def _():
-        meet([chip_neighbours(unit)[1], *group_neighbours(), *peers])
+    neighbours = [chip_neighbours(unit)[1], *group_neighbours(), *peers]
+
+    def greet():
+        meet(neighbours)
         for copy in rows_out:
             copy.start()
         for copies in over_y:
             for copy in copies:
                 copy.start()
 
+    load(step, load_sems, weights, greet)
     for holder, copy, _ in halo:
         pl.when((step == 0) & (half == 0) & (place == holder))(copy.start)
-    load(step, load_sems, weights)
 
     @pl.when(step == 0)
     def _():
@@ -547,6 +550,14 @@
                 copy.wait_recv()
             for copy in twice[k]:
                 copy.start()
+
+    for holder, copy, spread_copies in halo:
+
+        @pl.when((step == steps - 1) & (half == 1) & (place == holder))
+        def _():
+            copy.wait_recv()
+            for other in spread_copies:
+                other.start()
 
     x = xs_ref[...].astype(F32)
     center = x - jnp.mean(x, axis=-1, keepdims=True)
@@ -594,14 +605,6 @@
     @pl.when(step == steps - 1)
     def _():
         sums_ref[...] = acc_ref[...].astype(BF16)
-        for holder, copy, spread_copies in halo:
-
-            @pl.when((half == 1) & (place == holder))
-            def _():
-                copy.wait_recv()
-                for other in spread_copies:
-                    other.start()
-
         for holder, copy, spread_copies in halo:
             pl.when((half == 0) & (place == holder))(copy.wait_send)
 
@@ -774,16 +777,17 @@
                     for stage in stages:
                         stage[at]()
 
-    @pl.when(step == 0)
-    def _():
-        meet([*peers, y_peer] + ([net.x_peer, *net.z_peers] if hosted else []))
+    neighbours = [*peers, y_peer] + ([net.x_peer, *net.z_peers] if hosted else [])
+
+    def greet():
+        meet(neighbours)
         for ref in (norms_ref, output_right_grad_ref, down_right_grad_ref, acc_ref, up_left_grad_ref):
             ref[...] = jnp.zeros_like(ref)
 
+    load(step, load_sems, weights, greet)
     advance()
     for j, copy in enumerate(early_copies):
         pl.when(step == min(j + 1, steps - 1))(copy.start)
-    load(step, load_sems, weights)
     normed = normed_ref[...]
     low = low_ref[...]
     dy = dy_ref[...]
@@ -1279,9 +1283,10 @@
         ]
         for s, peer in enumerate(peers)
     ]
-    @pl.when(step == 0)
-    def _():
-        meet([y_peer, *peers])
+    neighbours = [y_peer, *peers]
+
+    def greet():
+        meet(neighbours)
 
         @pl.when(half == 1)
         def _():
@@ -1297,6 +1302,7 @@
             unit, (triple0_ref, triple1_ref), right_ref, (output0_ref, output1_ref), output_left_ref, triple_ref,
             output_ref,
         ),
+        greet,
     )
 
     key_ref[...], value_ref[...] = gk_ref[...], gv_ref[...]
@@ -1506,13 +1512,13 @@
 def unpack_kernel(triple_width, feed_ref, both_ref, heads_ref, left_ref, triple_ref, output_ref, up_ref, down_ref,
                   triple_left_ref, up_left_ref, output_right_ref, down_right_ref, *norm_refs):
     triple_ref[...] = heads_ref[0, 0, :, :triple_width].astype(F32)
-    output_ref[...] = heads_ref[0, 0, :, triple_width:].astype(F32).T
+    output_ref[...] = heads_ref[0, 0, :, triple_width:].T.astype(F32)
     hidden = up_ref.shape[1]
     up_ref[...] = feed_ref[0, 0, :, :hidden].astype(F32)
-    down_ref[...] = feed_ref[0, 0, :, hidden:].astype(F32).T
+    down_ref[...] = feed_ref[0, 0, :, hidden:].T.astype(F32)
     size = triple_left_ref.shape[0]
-    triple_left_ref[...] = left_ref[0, 0].astype(F32).T
-    up_left_ref[...] = both_ref[0, 0, :, :size].astype(F32).T
+    triple_left_ref[...] = left_ref[0, 0].T.astype(F32)
+    up_left_ref[...] = both_ref[0, 0, :, :size].T.astype(F32)
     output_right_ref[...] = both_ref[0, 0, :, size : 2 * size].astype(F32)
     down_right_ref[...] = both_ref[0, 0, :, 2 * size : 3 * size].astype(F32)
     for q, ref in enumerate(norm_refs):

time: 236 us -> 232 us (0.983)
  starting transfers between devices: 12 us -> 3.8 us
  Pallas kernels: 216 us -> 221 us
    pallas_call x1, Pallas kernels: 24.8 us -> 31.2 us  [attend(): pl.pallas_call(functools.partial(attend_kernel, blocks, head_width // LAN...]
    ppermute x1, starting transfers between devices: 7.68 us -> 1.55 us  [shards(): expand_other = lax.ppermute(expand_piece, 'dp', beside[0])]
    pallas_call x1, Pallas kernels: 43.3 us -> 47.9 us  [feed_second(): pl.pallas_call(functools.partial(feed_second_kernel, unit, tile), grid=(s...]
    pallas_call x1, Pallas kernels: 39.4 us -> 34.9 us  [settle(): pl.pallas_call(functools.partial(settle_kernel, unit, tile), grid=(steps,...]
    ppermute x1, starting transfers between devices: 3.61 us -> 1.13 us  [shards(): expand_piece = lax.ppermute(expand_half, 'mp', swap)]
  transfers between devices with their start and end apart: 4 -> 4, of which waited for: 0 -> 0; matrix products, arithmetic and copies ran while one was open for 1% -> 1% of each run, Pallas kernels for 36% -> 37%
where the time goes in v2:
time: 232 us
  Pallas kernels  221 us (95%)
  local copies, waits for them, and re-layouts  6.35 us (3%)
  starting transfers between devices  3.8 us (2%)
    pallas_call x1, Pallas kernels, feed_second(): pl.pallas_call(functools.partial(feed_second_kernel, unit, tile), grid=(s...  47.9 us
    pallas_call x1, Pallas kernels, sum_all(): pl.pallas_call(functools.partial(sum_kernel, size), out_shape=outs, in_sp...  43.8 us
    pallas_call x1, Pallas kernels, feed_first(): pl.pallas_call(functools.partial(feed_first_kernel, unit, tile), grid=(st...  36.3 us
    pallas_call x1, Pallas kernels, settle(): pl.pallas_call(functools.partial(settle_kernel, unit, tile), grid=(steps,...  34.9 us
    pallas_call x1, Pallas kernels, attend(): pl.pallas_call(functools.partial(attend_kernel, blocks, head_width // LAN...  31.2 us
    pallas_call x1, Pallas kernels, project(): pl.pallas_call(functools.partial(project_kernel, unit, main_tiles), grid=...  20.6 us
    pallas_call x1, Pallas kernels, unpack(): pl.pallas_call(functools.partial(unpack_kernel, triple_width), grid=(4,),...  6.28 us
    unnamed x18, local copies, waits for them, and re-layouts  5.42 us
  transfers between devices with their start and end apart: 4, of which 0 were waited for; matrix products, arithmetic and copies ran while one was open for 1% of the time, Pallas kernels for 37%

profile of v2, /device:TPU:1, one launch (start us, length us, event | category | flops | bytes accessed | tf_op | source)
XLA Modules:
  0.0 232.3 jit_solution(11797576750246509997)
XLA Ops:
  0.7 36.3 %feed_first.1 = (bf16[1536,1024]{1,0:T(8,128)(2,1)}, bf16[1536,1024]{1,0:T(8,128)(2,1)}, bf16[1536,1024]{1,0:T(8,128)(2,1)}, bf16[1536,128]{1,0:T(8,128)(2,1)}, ...) custom-call(bf16[768,1024]{1,0:T(8,128)(2,1)} %x_ref.3, ...), custom_call_target="tpu_custom_call" | custom-call | flops 1 | bytes 1 | tf_op jit(solution)/shard_map/feed_first/pallas_call | solution.py:646
  36.9 1.1 collective-permute-start
  38.1 0.4 collective-permute-start.1
  38.5 0.2 reduce-window_clone.1
  38.7 0.2 and_reduce_fusion
  38.9 0.1 dynamic_slice.3.conts_ref
  38.9 0.1 broadcast_in_dim.37
  39.0 0.1 reshape.78
  39.1 0.7 broadcast_in_dim.38.late_ref
  39.8 20.6 %project.1 = (bf16[1536,128]{1,0:T(8,128)(2,1)}, bf16[1536,512]{1,0:T(8,128)(2,1)}, bf16[2048,512]{1,0:T(8,128)(2,1)}, bf16[2048,512]{1,0:T(8,128)(2,1)}, bf16[1536,512]{1,0:T(8,128)(2,1)}) custom-call(bf16[512,1024]{1,0:T(8,128)(2,1)} %get-tuple-element.74.halo_ref, bf16[1536,1024]{1,0:T(8,128)(2,1)} %get-tuple-element.73.normed_ref, ...), custom_call_target="tpu_custom_call" | custom-call | flops 1 | bytes 1 | tf_op jit(solution)/shard_map/project/pallas_call | solution.py:1060
  60.4 31.2 %attend.1 = (bf16[1536,512]{1,0:T(8,128)(2,1)}, bf16[1536,512]{1,0:T(8,128)(2,1)}, bf16[1536,512]{1,0:T(8,128)(2,1)}, bf16[1536,512]{1,0:T(8,128)(2,1)}, bf16[2,512,512]{2,1,0:T(8,128)(2,1)}) custom-call(s32[3]{0:T(128)} %copy-done.6, bf16[1536,512]{1,0:T(8,128)(2,1)} %get-tuple-element.81.q_ref, bf16[2048,512]{1,0:T(8,128)(2,1)} %get-tuple-element.82.k_ref.kp_ref, ...), custom_call_target="tpu_custom_call" | custom-call | flops 1 | bytes 1 | tf_op jit(solution)/shard_map/attend/pallas_call | solution.py:1237
  91.6 0.0 copy-start.2
  91.7 1.6 collective-permute-start.2
  93.2 0.7 collective-permute-start.3
  93.9 34.9 %settle.1 = (f32[1536,1024]{1,0:T(8,128)}, bf16[768,1152]{1,0:T(8,128)(2,1)}, bf16[2,128,1024]{2,1,0:T(8,128)(2,1)}, bf16[2,2,128,256]{3,2,1,0:T(8,128)(2,1)}, bf16[1,768,1152]{2,1,0:T(8,128)(2,1)}) custom-call(bf16[1536,1024]{1,0:T(8,128)(2,1)} %get-tuple-element.73.normed_ref, bf16[1536,128]{1,0:T(8,128)(2,1)} %get-tuple-element.77.low_ref, ...), custom_call_target="tpu_custom_call" | custom-call | flops 1 | bytes 1 | tf_op jit(solution)/shard_map/settle/pallas_call | solution.py:1388
  128.9 0.0 copy-start.4
  128.9 0.9 copy-done.4
  129.8 0.3 copy-done.5
  130.2 47.9 %feed_second.1 = (bf16[768,1024]{1,0:T(8,128)(2,1)}, f32[768,1024]{1,0:T(8,128)}, bf16[128,2048]{1,0:T(8,128)(2,1)}, bf16[2,2,128,896]{3,2,1,0:T(8,128)(2,1)}, b...) custom-call(bf16[1536,1024]{1,0:T(8,128)(2,1)} %get-tuple-element.69.normed_ref, ...), custom_call_target="tpu_custom_call" | custom-call | flops 1 | bytes 1 | tf_op jit(solution)/shard_map/feed_second/pallas_call | solution.py:914
  178.1 43.8 %sum_all.1 = (bf16[2,2,2,4,16,2048]{5,4,3,2,1,0:T(8,128)(2,1)}, bf16[2,2,2,4,16,896]{5,4,3,2,1,0:T(8,128)(2,1)}, bf16[2,2,2,4,16,1024]{5,4,3,2,1,0:T(8,128)(2,1)}, bf16[2,2,2,4,16,256]{5,4,3,2,1,0:T(8,128)(2,1)}) custom-call(bf16[2,4,16,2048]{3,2,1,0:T(8,128)(2,1)} %bitcast.25, bf16[2,2,2,4,16,896]{5,4,3,2,1,0:T(8,128)(2,1)} %bitcast.23, ...), custom_call_target="tpu_custom_call" | custom-call | flops 1 | bytes 1 | tf_op jit(solution)/shard_map/sum_all/pallas_call | solution.py:1495
  221.9 6.3 %unpack.1 = (f32[128,3072]{1,0:T(8,128)}, f32[1024,128]{1,0:T(8,128)}, f32[128,4096]{1,0:T(8,128)}, f32[4096,128]{1,0:T(8,128)}, f32[1024,128]{1,0:T(8,128)}, /*...) custom-call(bf16[2,2,128,2048]{3,2,1,0:T(8,128)(2,1)} %bitcast.20, ...), custom_call_target="tpu_custom_call" | custom-call | flops 1 | bytes 1 | tf_op jit(solution)/shard_map/unpack/pallas_call | solution.py:1542
  228.2 1.1 copy.40
  229.3 1.3 copy-done
  230.6 1.7 copy.41
  (20 shorter events, 0.1 us)
Async XLA Ops:
  0.6 37.8 %copy-start.7 = (s32[1,6]{1,0:T(1,128)S(1)}, s32[1,6]{1,0:T(1,128)}, u32[]{:S(2)}) copy-start(s32[1,6]{1,0:T(1,128)} %param.25) | copy-start | bytes 76
  36.9 54.7 %collective-permute-start = (bf16[512,1024]{1,0:T(8,128)(2,1)}, bf16[512,1024]{1,0:T(8,128)(2,1)S(1)}, u32[]{:S(2)}, u32[]{:S(2)}) collective-permute-start(bf16[512,1024]{1,0:T(8,128)(2,1)} %get-tuple-element.79), channel_id=1, source_target_pairs={{0,2},{1,3},{2,0},{3,1},{4,6},{5,7},{6,4},{7,5},{8,10},{9,11},{10,... | collective-permute-start | bytes 3145736 | tf_op jit(solution)/shard_map/ppermute | solution.py:1618
  38.1 53.6 %collective-permute-start.1 = (bf16[512,1024]{1,0:T(8,128)(2,1)}, bf16[512,1024]{1,0:T(8,128)(2,1)S(1)}, u32[]{:S(2)}, u32[]{:S(2)}) collective-permute-start(bf16[512,1024]{1,0:T(8,128)(2,1)} %get-tuple-element.80), channel_id=1, source_target_pairs={{0,2},{1,3},{2,0},{3,1},{4,6},{5,7},{6,4},{7,5},{8,10},{9,11},{10,... | collective-permute-start | bytes 3145736 | tf_op jit(solution)/shard_map/ppermute | solution.py:1619
  38.9 21.4 %copy-start.6 = (s32[3]{0:T(128)}, s32[3]{0:T(128)S(1)}, u32[]{:S(2)}) copy-start(s32[3]{0:T(128)S(1)} %dynamic_slice.3.conts_ref) | copy-start | bytes 40
  91.6 37.2 %copy-start.2 = (bf16[512,1024]{1,0:T(8,128)(2,1)}, bf16[512,1024]{1,0:T(8,128)(2,1)S(1)}, u32[]{:S(2)}) copy-start(bf16[512,1024]{1,0:T(8,128)(2,1)S(1)} %collective-permute-done.up0_ref) | copy-start | bytes 3145732
  91.7 37.2 %copy-start.3 = (bf16[512,1024]{1,0:T(8,128)(2,1)}, bf16[512,1024]{1,0:T(8,128)(2,1)S(1)}, u32[]{:S(2)}) copy-start(bf16[512,1024]{1,0:T(8,128)(2,1)S(1)} %collective-permute-done.1.down0_ref) | copy-start | bytes 3145732
  91.7 37.2 %collective-permute-start.2 = (bf16[512,1024]{1,0:T(8,128)(2,1)S(1)}, bf16[512,1024]{1,0:T(8,128)(2,1)S(1)}, u32[]{:S(2)}, u32[]{:S(2)}) collective-permute-start(bf16[512,1024]{1,0:T(8,128)(2,1)S(1)} %collective-permute-done.up0_ref), channel_id=1, source_target_pairs={{0,4},{4,0},{8,12},{12,8},{16,20},{20,16},{24,28},{28,24},{1,5},{5... | collective-permute-start | bytes 3145736 | tf_op jit(solution)/shard_map/ppermute | solution.py:1626
  93.2 35.6 %collective-permute-start.3 = (bf16[512,1024]{1,0:T(8,128)(2,1)S(1)}, bf16[512,1024]{1,0:T(8,128)(2,1)S(1)}, u32[]{:S(2)}, u32[]{:S(2)}) collective-permute-start(bf16[512,1024]{1,0:T(8,128)(2,1)S(1)} %collective-permute-done.1.down0_ref), channel_id=1, source_target_pairs={{0,8},{4,12},{8,0},{12,4},{16,24},{20,28},{24,16},{28,20},{1,9},{5... | collective-permute-start | bytes 3145736 | tf_op jit(solution)/shard_map/ppermute | solution.py:1627
  128.9 1.0 copy-start.4
  128.9 1.3 copy-start.5
  221.9 6.3 %copy-start.1 = (bf16[768,1024]{1,0:T(8,128)(2,1)S(1)}, bf16[768,1024]{1,0:T(8,128)(2,1)}, u32[]{:S(2)}) copy-start(bf16[768,1024]{1,0:T(8,128)(2,1)} %get-tuple-element.138) | copy-start | bytes 4718596
  228.2 2.5 %copy-start = (f32[768,1024]{1,0:T(8,128)S(1)}, f32[768,1024]{1,0:T(8,128)}, u32[]{:S(2)}) copy-start(f32[768,1024]{1,0:T(8,128)} %get-tuple-element.139) | copy-start | bytes 9437188

commit v3 on v2

--- a/solution.py
+++ b/solution.py
@@ -1511,21 +1511,26 @@
 
 def unpack_kernel(triple_width, feed_ref, both_ref, heads_ref, left_ref, triple_ref, output_ref, up_ref, down_ref,
                   triple_left_ref, up_left_ref, output_right_ref, down_right_ref, *norm_refs):
-    triple_ref[...] = heads_ref[0, 0, :, :triple_width].astype(F32)
-    output_ref[...] = heads_ref[0, 0, :, triple_width:].T.astype(F32)
+    part = pl.program_id(1)
+
+    def columns(ref, start, size):
+        return ref[0, 0, :, pl.ds(pl.multiple_of(start + part * size, LANES), size)]
+
+    triple_ref[...] = columns(heads_ref, 0, triple_ref.shape[1]).astype(F32)
+    output_ref[...] = columns(heads_ref, triple_width, output_ref.shape[0]).T.astype(F32)
     hidden = up_ref.shape[1]
-    up_ref[...] = feed_ref[0, 0, :, :hidden].astype(F32)
-    down_ref[...] = feed_ref[0, 0, :, hidden:].T.astype(F32)
+    up_ref[...] = columns(feed_ref, 0, hidden).astype(F32)
+    down_ref[...] = columns(feed_ref, 2 * hidden, hidden).T.astype(F32)
     size = triple_left_ref.shape[0]
-    triple_left_ref[...] = left_ref[0, 0].T.astype(F32)
-    up_left_ref[...] = both_ref[0, 0, :, :size].T.astype(F32)
-    output_right_ref[...] = both_ref[0, 0, :, size : 2 * size].astype(F32)
-    down_right_ref[...] = both_ref[0, 0, :, 2 * size : 3 * size].astype(F32)
+    triple_left_ref[...] = columns(left_ref, 0, size).T.astype(F32)
+    up_left_ref[...] = columns(both_ref, 0, size).T.astype(F32)
+    output_right_ref[...] = columns(both_ref, 2 * size, size).astype(F32)
+    down_right_ref[...] = columns(both_ref, 4 * size, size).astype(F32)
     for q, ref in enumerate(norm_refs):
 
-        @pl.when(pl.program_id(0) == q)
+        @pl.when((pl.program_id(0) == q) & (part == 0))
         def _():
-            ref[...] = both_ref[0, 0, : ref.shape[0], 3 * size :].astype(F32)
+            ref[...] = both_ref[0, 0, : ref.shape[0], 6 * size :].astype(F32)
 
 
 def unpack(feed, both, heads, left, triple_width):
@@ -1534,16 +1539,16 @@
     width, head_width = 4 * quarter, heads.shape[-1] - triple_width
 
     def tall(rows):
-        return pl.BlockSpec((rows, LANES), lambda s: (s, 0))
+        return pl.BlockSpec((rows // 2, LANES), lambda s, part: (2 * s + part, 0))
 
     def wide(cols):
-        return pl.BlockSpec((LANES, cols), lambda s: (0, s))
+        return pl.BlockSpec((LANES, cols // 2), lambda s, part: (0, 2 * s + part))
 
     return pl.pallas_call(
         functools.partial(unpack_kernel, triple_width),
-        grid=(4,),
+        grid=(4, 2),
         in_specs=[
-            pl.BlockSpec((1, 1) + value.shape[2:], lambda s: (lax.rem(s, 2), s // 2, 0, 0)) for value in arrays
+            pl.BlockSpec((1, 1) + value.shape[2:], lambda s, part: (lax.rem(s, 2), s // 2, 0, 0)) for value in arrays
         ],
         out_specs=[
             wide(triple_width), tall(head_width), wide(hidden), tall(hidden), tall(quarter), tall(quarter),
@@ -1560,7 +1565,7 @@
             shaped((LANES, width), F32),
         ]
         + [shaped((width // LANES, LANES), F32)] * 4,
-        compiler_params=params(),
+        compiler_params=params(2),
         cost_estimate=BRIEF,
         name="unpack",
     )(*arrays)

time: 232 us -> 235 us (1.013)
    pallas_call x1, Pallas kernels: 47.9 us -> 42.6 us  [feed_second(): pl.pallas_call(functools.partial(feed_second_kernel, unit, tile), grid=(s...]
    pallas_call x1, Pallas kernels: 34.9 us -> 39.9 us  [settle(): pl.pallas_call(functools.partial(settle_kernel, unit, tile), grid=(steps,...]
    pallas_call x1, Pallas kernels: 6.28 us -> 9.33 us  [unpack(): pl.pallas_call(functools.partial(unpack_kernel, triple_width), grid=(4, 2...]
  transfers between devices with their start and end apart: 4 -> 4, of which waited for: 0 -> 0; matrix products, arithmetic and copies ran while one was open for 1% -> 1% of each run, Pallas kernels for 37% -> 39%
where the time goes in v3:
time: 235 us; the launch traced here: 234 us
  Pallas kernels  222 us (94%)
  local copies, waits for them, and re-layouts  6.35 us (3%)
  starting transfers between devices  3.8 us (2%)
    pallas_call x1, Pallas kernels, feed_second(): pl.pallas_call(functools.partial(feed_second_kernel, unit, tile), grid=(s...  42.6 us
    pallas_call x1, Pallas kernels, sum_all(): pl.pallas_call(functools.partial(sum_kernel, size), out_shape=outs, in_sp...  42.3 us
    pallas_call x1, Pallas kernels, settle(): pl.pallas_call(functools.partial(settle_kernel, unit, tile), grid=(steps,...  39.9 us
    pallas_call x1, Pallas kernels, feed_first(): pl.pallas_call(functools.partial(feed_first_kernel, unit, tile), grid=(st...  36.3 us
    pallas_call x1, Pallas kernels, attend(): pl.pallas_call(functools.partial(attend_kernel, blocks, head_width // LAN...  31.2 us
    pallas_call x1, Pallas kernels, project(): pl.pallas_call(functools.partial(project_kernel, unit, main_tiles), grid=...  20.6 us
    pallas_call x1, Pallas kernels, unpack(): pl.pallas_call(functools.partial(unpack_kernel, triple_width), grid=(4, 2...  9.33 us
    unnamed x18, local copies, waits for them, and re-layouts  5.42 us
  transfers between devices with their start and end apart: 4, of which 0 were waited for; matrix products, arithmetic and copies ran while one was open for 1% of the time, Pallas kernels for 39%

profile of v3, /device:TPU:1, one launch (start us, length us, event | category | flops | bytes accessed | tf_op | source)
XLA Modules:
  0.0 233.6 jit_solution(11422217327822725651)
XLA Ops:
  0.7 36.3 %feed_first.1 = (bf16[1536,1024]{1,0:T(8,128)(2,1)}, bf16[1536,1024]{1,0:T(8,128)(2,1)}, bf16[1536,1024]{1,0:T(8,128)(2,1)}, bf16[1536,128]{1,0:T(8,128)(2,1)}, ...) custom-call(bf16[768,1024]{1,0:T(8,128)(2,1)} %x_ref.3, ...), custom_call_target="tpu_custom_call" | custom-call | flops 1 | bytes 1 | tf_op jit(solution)/shard_map/feed_first/pallas_call | solution.py:646
  36.9 1.1 collective-permute-start
  38.1 0.4 collective-permute-start.1
  38.5 0.2 reduce-window_clone.1
  38.7 0.2 and_reduce_fusion
  38.9 0.1 dynamic_slice.3.conts_ref
  38.9 0.1 broadcast_in_dim.37
  39.0 0.1 reshape.78
  39.1 0.7 broadcast_in_dim.38.late_ref
  39.8 20.6 %project.1 = (bf16[1536,128]{1,0:T(8,128)(2,1)}, bf16[1536,512]{1,0:T(8,128)(2,1)}, bf16[2048,512]{1,0:T(8,128)(2,1)}, bf16[2048,512]{1,0:T(8,128)(2,1)}, bf16[1536,512]{1,0:T(8,128)(2,1)}) custom-call(bf16[512,1024]{1,0:T(8,128)(2,1)} %get-tuple-element.74.halo_ref, bf16[1536,1024]{1,0:T(8,128)(2,1)} %get-tuple-element.73.normed_ref, ...), custom_call_target="tpu_custom_call" | custom-call | flops 1 | bytes 1 | tf_op jit(solution)/shard_map/project/pallas_call | solution.py:1060
  60.4 31.2 %attend.1 = (bf16[1536,512]{1,0:T(8,128)(2,1)}, bf16[1536,512]{1,0:T(8,128)(2,1)}, bf16[1536,512]{1,0:T(8,128)(2,1)}, bf16[1536,512]{1,0:T(8,128)(2,1)}, bf16[2,512,512]{2,1,0:T(8,128)(2,1)}) custom-call(s32[3]{0:T(128)} %copy-done.6, bf16[1536,512]{1,0:T(8,128)(2,1)} %get-tuple-element.81.q_ref, bf16[2048,512]{1,0:T(8,128)(2,1)} %get-tuple-element.82.k_ref.kp_ref, ...), custom_call_target="tpu_custom_call" | custom-call | flops 1 | bytes 1 | tf_op jit(solution)/shard_map/attend/pallas_call | solution.py:1237
  91.6 0.0 copy-start.2
  91.7 0.0 copy-start.3
  91.7 1.6 collective-permute-start.2
  93.2 0.7 collective-permute-start.3
  93.9 39.9 %settle.1 = (f32[1536,1024]{1,0:T(8,128)}, bf16[768,1152]{1,0:T(8,128)(2,1)}, bf16[2,128,1024]{2,1,0:T(8,128)(2,1)}, bf16[2,2,128,256]{3,2,1,0:T(8,128)(2,1)}, bf16[1,768,1152]{2,1,0:T(8,128)(2,1)}) custom-call(bf16[1536,1024]{1,0:T(8,128)(2,1)} %get-tuple-element.73.normed_ref, bf16[1536,128]{1,0:T(8,128)(2,1)} %get-tuple-element.77.low_ref, ...), custom_call_target="tpu_custom_call" | custom-call | flops 1 | bytes 1 | tf_op jit(solution)/shard_map/settle/pallas_call | solution.py:1388
  133.9 0.9 copy-done.4
  134.8 0.3 copy-done.5
  135.2 42.6 %feed_second.1 = (bf16[768,1024]{1,0:T(8,128)(2,1)}, f32[768,1024]{1,0:T(8,128)}, bf16[128,2048]{1,0:T(8,128)(2,1)}, bf16[2,2,128,896]{3,2,1,0:T(8,128)(2,1)}, b...) custom-call(bf16[1536,1024]{1,0:T(8,128)(2,1)} %get-tuple-element.69.normed_ref, ...), custom_call_target="tpu_custom_call" | custom-call | flops 1 | bytes 1 | tf_op jit(solution)/shard_map/feed_second/pallas_call | solution.py:914
  177.8 42.3 %sum_all.1 = (bf16[2,2,2,4,16,2048]{5,4,3,2,1,0:T(8,128)(2,1)}, bf16[2,2,2,4,16,896]{5,4,3,2,1,0:T(8,128)(2,1)}, bf16[2,2,2,4,16,1024]{5,4,3,2,1,0:T(8,128)(2,1)}, bf16[2,2,2,4,16,256]{5,4,3,2,1,0:T(8,128)(2,1)}) custom-call(bf16[2,4,16,2048]{3,2,1,0:T(8,128)(2,1)} %bitcast.25, bf16[2,2,2,4,16,896]{5,4,3,2,1,0:T(8,128)(2,1)} %bitcast.23, ...), custom_call_target="tpu_custom_call" | custom-call | flops 1 | bytes 1 | tf_op jit(solution)/shard_map/sum_all/pallas_call | solution.py:1495
  220.1 9.3 %unpack.1 = (f32[128,3072]{1,0:T(8,128)}, f32[1024,128]{1,0:T(8,128)}, f32[128,4096]{1,0:T(8,128)}, f32[4096,128]{1,0:T(8,128)}, f32[1024,128]{1,0:T(8,128)}, /*...) custom-call(bf16[2,2,128,2048]{3,2,1,0:T(8,128)(2,1)} %bitcast.20, ...), custom_call_target="tpu_custom_call" | custom-call | flops 1 | bytes 1 | tf_op jit(solution)/shard_map/unpack/pallas_call | solution.py:1547
  229.5 1.1 copy.40
  230.6 1.3 copy-done
  231.9 1.7 copy.41
  (20 shorter events, 0.1 us)
Async XLA Ops:
  0.6 37.8 %copy-start.7 = (s32[1,6]{1,0:T(1,128)S(1)}, s32[1,6]{1,0:T(1,128)}, u32[]{:S(2)}) copy-start(s32[1,6]{1,0:T(1,128)} %param.25) | copy-start | bytes 76
  36.9 54.7 %collective-permute-start = (bf16[512,1024]{1,0:T(8,128)(2,1)}, bf16[512,1024]{1,0:T(8,128)(2,1)S(1)}, u32[]{:S(2)}, u32[]{:S(2)}) collective-permute-start(bf16[512,1024]{1,0:T(8,128)(2,1)} %get-tuple-element.79), channel_id=1, source_target_pairs={{0,2},{1,3},{2,0},{3,1},{4,6},{5,7},{6,4},{7,5},{8,10},{9,11},{10,... | collective-permute-start | bytes 3145736 | tf_op jit(solution)/shard_map/ppermute | solution.py:1623
  38.1 53.6 %collective-permute-start.1 = (bf16[512,1024]{1,0:T(8,128)(2,1)}, bf16[512,1024]{1,0:T(8,128)(2,1)S(1)}, u32[]{:S(2)}, u32[]{:S(2)}) collective-permute-start(bf16[512,1024]{1,0:T(8,128)(2,1)} %get-tuple-element.80), channel_id=1, source_target_pairs={{0,2},{1,3},{2,0},{3,1},{4,6},{5,7},{6,4},{7,5},{8,10},{9,11},{10,... | collective-permute-start | bytes 3145736 | tf_op jit(solution)/shard_map/ppermute | solution.py:1624
  38.9 21.4 %copy-start.6 = (s32[3]{0:T(128)}, s32[3]{0:T(128)S(1)}, u32[]{:S(2)}) copy-start(s32[3]{0:T(128)S(1)} %dynamic_slice.3.conts_ref) | copy-start | bytes 40
  91.6 42.2 %copy-start.2 = (bf16[512,1024]{1,0:T(8,128)(2,1)}, bf16[512,1024]{1,0:T(8,128)(2,1)S(1)}, u32[]{:S(2)}) copy-start(bf16[512,1024]{1,0:T(8,128)(2,1)S(1)} %collective-permute-done.up0_ref) | copy-start | bytes 3145732
  91.7 42.2 %copy-start.3 = (bf16[512,1024]{1,0:T(8,128)(2,1)}, bf16[512,1024]{1,0:T(8,128)(2,1)S(1)}, u32[]{:S(2)}) copy-start(bf16[512,1024]{1,0:T(8,128)(2,1)S(1)} %collective-permute-done.1.down0_ref) | copy-start | bytes 3145732
  91.7 42.2 %collective-permute-start.2 = (bf16[512,1024]{1,0:T(8,128)(2,1)S(1)}, bf16[512,1024]{1,0:T(8,128)(2,1)S(1)}, u32[]{:S(2)}, u32[]{:S(2)}) collective-permute-start(bf16[512,1024]{1,0:T(8,128)(2,1)S(1)} %collective-permute-done.up0_ref), channel_id=1, source_target_pairs={{0,4},{4,0},{8,12},{12,8},{16,20},{20,16},{24,28},{28,24},{1,5},{5... | collective-permute-start | bytes 3145736 | tf_op jit(solution)/shard_map/ppermute | solution.py:1631
  93.2 40.6 %collective-permute-start.3 = (bf16[512,1024]{1,0:T(8,128)(2,1)S(1)}, bf16[512,1024]{1,0:T(8,128)(2,1)S(1)}, u32[]{:S(2)}, u32[]{:S(2)}) collective-permute-start(bf16[512,1024]{1,0:T(8,128)(2,1)S(1)} %collective-permute-done.1.down0_ref), channel_id=1, source_target_pairs={{0,8},{4,12},{8,0},{12,4},{16,24},{20,28},{24,16},{28,20},{1,9},{5... | collective-permute-start | bytes 3145736 | tf_op jit(solution)/shard_map/ppermute | solution.py:1632
  133.9 1.0 copy-start.4
  133.9 1.3 copy-start.5
  220.1 9.4 %copy-start.1 = (bf16[768,1024]{1,0:T(8,128)(2,1)S(1)}, bf16[768,1024]{1,0:T(8,128)(2,1)}, u32[]{:S(2)}) copy-start(bf16[768,1024]{1,0:T(8,128)(2,1)} %get-tuple-element.138) | copy-start | bytes 4718596
  229.5 2.5 %copy-start = (f32[768,1024]{1,0:T(8,128)S(1)}, f32[768,1024]{1,0:T(8,128)}, u32[]{:S(2)}) copy-start(f32[768,1024]{1,0:T(8,128)} %get-tuple-element.139) | copy-start | bytes 9437188
